TPU v7x, 32 devices: a whole 2x2x4 slice. The times are simulated.
32 devices in a mesh: rep: 16 (over z, y, x), tp: 2 (over core).
Axes of the slice: x: 2, y: 2, z: 4, core: 2. Of those that a mesh axis runs over, the one named last changes fastest.
Arguments:
- hidden: bfloat16 [512, 4, 5120], P('rep', None, 'tp'), may hold values from -6 to 6
- queries: bfloat16 [512, 4, 8192], P('rep', None, 'tp'), may hold values from -128 to 128
- key_cache: bfloat16 [512, 256, 1024], P('rep', None, 'tp'), may hold values from -4 to 4
- value_cache: bfloat16 [512, 256, 1024], P('rep', None, 'tp'), may hold values from -4 to 4
- lengths: int32 [512], P('rep'), may hold values from 2 to 256, as said below
- adopt: int32 [16], P('rep'), may hold values from 0 to 4
- old_kv: bfloat16 [5120, 2, 1024], P(None, None, 'tp'), may hold values from -0.078125 to 0.078125
- fresh_kv: bfloat16 [5120, 2, 1024], P('rep', None, 'tp'), may hold values from -0.078125 to 0.078125
Outputs:
- attended: bfloat16 [512, 4, 8192], P('rep', None, 'tp')
- appended: bfloat16 [512, 4, 2, 1024], P('rep', None, None, 'tp')
Inputs may be any that keep to these rules, and one draw needn't show every extreme that they name: `lengths`: each replica's block of 32 rows has a row with 256 cached tokens.
All inputs are finite; a program needn't handle non-finite values.
Results may differ from a plain program's by a relative error of at most 0.0053.
Values may be sent and summed in bfloat16 or wider, within the bound.
A program may use at most 192 MiB of HBM per device.

v0:
```python
import jax
import jax.numpy as jnp
from jax import lax
from jax.sharding import PartitionSpec as P

HEAD = 128


epsilon = 1e-06


def attend(queries, key_cache, value_cache, lengths, fresh_keys, fresh_values):
    row_count = queries.shape[0]
    step_count = queries.shape[1]
    head_count = fresh_keys.shape[2]
    depth = fresh_keys.shape[3]
    context = key_cache.shape[1]
    grouped = queries.reshape(row_count, step_count, head_count, -1, depth)
    cached_keys = key_cache.reshape(row_count, context, head_count, depth)
    cached_values = value_cache.reshape(row_count, context, head_count, depth)
    scaling = depth ** (-0.5)
    cache_scores = (
        jnp.einsum("rshgd,rthd->rshgt", grouped, cached_keys, preferred_element_type=jnp.float32)
        * scaling
    )
    fresh_scores = (
        jnp.einsum("rshgd,rphd->rshgp", grouped, fresh_keys, preferred_element_type=jnp.float32)
        * scaling
    )
    visible_cache = (jnp.arange(context, dtype=jnp.int32)[None, :] < lengths[:, None])[
        :, None, None, None, :
    ]
    stepping = jnp.arange(step_count, dtype=jnp.int32)
    visible_fresh = (stepping[None, :] <= stepping[:, None])[None, :, None, None, :]
    cache_scores = jnp.where(visible_cache, cache_scores, -1e30)
    fresh_scores = jnp.where(visible_fresh, fresh_scores, -1e30)
    highest = jnp.maximum(
        jnp.max(cache_scores, axis=-1, keepdims=True), jnp.max(fresh_scores, axis=-1, keepdims=True)
    )
    cache_weights = jnp.where(visible_cache, jnp.exp(cache_scores - highest), 0.0)
    fresh_weights = jnp.where(visible_fresh, jnp.exp(fresh_scores - highest), 0.0)
    denominator = jnp.sum(cache_weights, axis=-1, keepdims=True) + jnp.sum(
        fresh_weights, axis=-1, keepdims=True
    )
    cache_probs = (cache_weights / denominator).astype(jnp.bfloat16)
    fresh_probs = (fresh_weights / denominator).astype(jnp.bfloat16)
    mixed = jnp.einsum(
        "rshgt,rthd->rshgd", cache_probs, cached_values, preferred_element_type=jnp.float32
    )
    mixed = mixed + jnp.einsum(
        "rshgp,rphd->rshgd", fresh_probs, fresh_values, preferred_element_type=jnp.float32
    )
    return mixed.reshape(row_count, step_count, -1).astype(jnp.bfloat16)


def on_device(hidden, queries, key_cache, value_cache, lengths, adopt, old_kv, fresh_kv):
    gathered = lax.all_gather(hidden, "tp", axis=2, tiled=True)
    widened = gathered.astype(jnp.float32)
    normed = (
        widened * lax.rsqrt(jnp.mean(widened * widened, axis=-1, keepdims=True) + epsilon)
    ).astype(jnp.bfloat16)
    row_count = normed.shape[0]
    step_count = normed.shape[1]
    feature_count = normed.shape[2]
    local_width = old_kv.shape[2]
    flattened = normed.reshape(row_count * step_count, feature_count)
    stale = jnp.dot(
        flattened,
        old_kv.reshape(feature_count, 2 * local_width),
        preferred_element_type=jnp.float32,
    )
    weight_piece = fresh_kv.reshape(fresh_kv.shape[0], 2 * local_width)
    weights_whole = lax.all_gather(weight_piece, "rep", axis=0, tiled=True)
    current = jnp.dot(flattened, weights_whole, preferred_element_type=jnp.float32)
    use_fresh = jnp.arange(step_count, dtype=jnp.int32) >= adopt[0]
    chosen = jnp.where(
        use_fresh[None, :, None],
        current.reshape(row_count, step_count, 2 * local_width),
        stale.reshape(row_count, step_count, 2 * local_width),
    )
    head_count = local_width // HEAD
    chosen = chosen.reshape(row_count, step_count, 2, head_count, HEAD)
    new_keys = chosen[:, :, 0]
    new_values = chosen[:, :, 1]
    new_keys = new_keys * lax.rsqrt(jnp.mean(new_keys * new_keys, axis=-1, keepdims=True) + epsilon)
    appended = jnp.stack([new_keys, new_values], axis=2).astype(jnp.bfloat16)
    attended = attend(
        queries, key_cache, value_cache, lengths, appended[:, :, 0], appended[:, :, 1]
    )
    return (attended, appended.reshape(row_count, step_count, 2, local_width))


def solution(mesh):
    placed = (
        P("rep", None, "tp"),
        P("rep", None, "tp"),
        P("rep", None, "tp"),
        P("rep", None, "tp"),
        P("rep"),
        P("rep"),
        P(None, None, "tp"),
        P("rep", None, "tp"),
    )
    return jax.shard_map(
        on_device,
        mesh=mesh,
        in_specs=placed,
        out_specs=(P("rep", None, "tp"), P("rep", None, None, "tp")),
        check_vma=False,
    )
```

profile of v0, /device:TPU:0, one launch (start us, length us, event | category | flops | bytes accessed | tf_op | source)
XLA Modules:
  0.0 195.2 jit_solution(1064763748185675882)
XLA Ops:
  7.2 0.7 all-gather.3.cloned.1.call-update
  7.9 0.0 all-gather.5.cloned.1.call-start
  7.9 2.0 %copy.75 = bf16[40,8,2,512]{3,1,2,0:T(8,128)(2,1)} copy(bf16[40,8,2,512]{3,2,1,0:T(2,128)(2,1)} %bitcast.61) | data formatting | bytes 1310720
  10.0 17.8 %reshape.106 = bf16[5120,1024,1]{1,0,2:T(8,128)(2,1)} reshape(bf16[5120,2,512]{2,1,0:T(2,128)(2,1)} %param.14) | data formatting | bytes 20971520 | tf_op jit(solution)/shard_map/reshape | solution.py:69
  28.5 1.1 reshape.99
  29.6 12.6 %reshape.98 = bf16[32,256,4,128]{3,2,1,0:T(4,128)(2,1)} reshape(bf16[32,256,512]{2,1,0:T(8,128)(2,1)} %param.10) | data formatting | bytes 16777216 | tf_op jit(solution)/shard_map/reshape | solution.py:19
  42.2 12.6 %reshape.103 = bf16[32,256,4,128]{3,2,1,0:T(4,128)(2,1)} reshape(bf16[32,256,512]{2,1,0:T(8,128)(2,1)} %param.11) | data formatting | bytes 16777216 | tf_op jit(solution)/shard_map/reshape | solution.py:20
  54.8 0.1 iota_compare_fusion
  54.9 8.4 %bitcast_reduce_fusion = (f32[32,4,4,8]{3,1,2,0:T(4,128)S(1)}, f32[32,4,256,4,8]{2,4,3,1,0:T(8,128)}) fusion(pred[32,256]{1,0:T(8,128)(4,1)S(1)} %iota_compare_fusion, bf16[32,4,4,8,128]{4,3,2,1,0:T(8,128)(2,1)S(1)} %reshape.99, bf16[32,256,4,128,1]{3,2,1,0,4:T(4,128)(2,1)} %bitcast.59), kind=kOutput, calls=%fused_computation.7 | convolution fusion | flops 271577088 | bytes 13656064 | tf_op jit(solution)/shard_map/rshgd,rthd->rshgt/dot_general | solution.py:23
  63.3 2.1 %fusion.9 = f32[32,4]{1,0:T(8,128)S(1)} fusion(bf16[32,4,5120]{2,1,0:T(4,128)(2,1)} %all-gather.3.cloned.1.call-done), kind=kLoop, calls=%fused_computation.15 | loop fusion | flops 1965952 | bytes 1311232 | tf_op jit(solution)/shard_map/reduce_sum | solution.py:60
  65.4 1.9 fusion.10
  67.4 91.0 %all-gather.5.cloned.1.call-done = bf16[5120,1024]{1,0:T(8,128)(2,1)} async-done(((bf16[320,1024]{1,0:T(8,128)(2,1)}), bf16[5120,1024]{1,0:T(8,128)(2,1)}) %all-gather.5.cloned.1.call-update) | async-done | bytes 10485776 | tf_op jit(solution)/shard_map/all_gather | solution.py:73
  158.4 5.8 %fusion = f32[32,4,1024]{2,0,1:T(8,128)S(1)} fusion(bf16[5120,1024]{1,0:T(8,128)(2,1)} %all-gather.5.cloned.1.call-done, bf16[32,4,5120]{2,1,0:T(4,128)(2,1)S(1)} %fusion.10), kind=kOutput, calls=%fused_computation | convolution fusion | flops 1342177280 | bytes 12320768 | tf_op jit(solution)/shard_map/dot_general | solution.py:74
  164.2 5.8 %convolution_select_fusion = f32[32,4,1024]{2,0,1:T(8,128)S(1)} fusion(f32[32,4,1024]{2,0,1:T(8,128)S(1)} %fusion, bf16[5120,1024,1]{1,0,2:T(8,128)(2,1)} %reshape.106, bf16[32,4,5120]{2,1,0:T(4,128)(2,1)S(1)} %fusion.10, pred[4]{0:T(512)(128)(4,1)S(1)} %iota_compare_fusion.2), kind=kOutput, calls=%fused_computation.29 | convolution fusion | flops 1342308352 | bytes 12845060 | tf_op jit(solution)/shard_map/dot_general | solution.py:67
  169.9 0.2 reshape.102
  170.2 0.2 multiply_reduce_fusion
  170.5 0.2 fusion.39
  170.7 0.2 multiply_convert_fusion
  170.9 4.8 %fusion.36 = (f32[32,4,4,8]{3,1,2,0:T(4,128)S(1)}, f32[32,4,4,8,4]{3,4,1,2,0:T(4,128)S(1)}) fusion(bf16[32,4,4,8,128]{4,3,2,1,0:T(8,128)(2,1)S(1)} %reshape.99, bf16[32,4,4,128,1]{3,2,0,1,4:T(4,128)(2,1)S(1)} %fusion.39, pred[4,4]{1,0:T(4,128)(4,1)S(1)} %iota_compare_fusion.1), kind=kOutput, calls=%fused_computation.57 | convolution fusion | flops 4239360 | bytes 1261584 | tf_op jit(solution)/shard_map/rshgd,rphd->rshgp/dot_general | solution.py:27
  175.7 0.1 max.8
  175.8 1.2 fusion.25
  177.0 1.8 fusion.8
  178.8 0.1 copy.92
  178.9 0.1 add.37
  179.0 5.8 %fusion.2 = f32[32,4,4,8,128]{4,3,2,1,0:T(8,128)S(1)} fusion(bf16[32,256,4,128,1]{3,2,1,0,4:T(4,128)(2,1)} %bitcast.58, f32[32,4,256,4,8]{2,4,3,1,0:T(8,128)S(1)} %copy-done, f32[32,4,4,8]{3,1,2,0:T(4,128)S(1)} %add.37, f32[32,4,4,8]{3,1,2,0:T(4,128)S(1)} %max.8, pred[32,256]{1,0:T(8,128)(4,1)S(1)} %iota_compare_fusion), kind=kOutput, calls=%fused_computation.2 | convolution fusion | flops 274726912 | bytes 14721024 | tf_op jit(solution)/shard_map/rshgt,rthd->rshgd/dot_general | solution.py:47
  184.8 1.0 fusion.11
  185.8 0.2 copy.71
  186.0 1.1 reshape.111
  187.1 0.1 stack.9
  187.2 0.1 copy.58
  187.3 0.1 stack.10
  187.4 1.0 copy.60
  (15 shorter events, 0.2 us)
Async XLA Ops:
  7.2 56.2 %all-gather.3.cloned.1.call-start = ((), (), s32[]{:S(2)}) async-start(), calls=%async_computation | async-start | bytes 1966080 | tf_op jit(solution)/shard_map/all_gather | solution.py:57
  7.9 150.5 %all-gather.5.cloned.1.call-start = ((), (), s32[]{:S(2)}) async-start(), calls=%async_computation.1 | async-start | bytes 11141120 | tf_op jit(solution)/shard_map/all_gather | solution.py:73
  10.0 18.5 %copy-start.1 = (bf16[32,4,4096]{2,1,0:T(4,128)(2,1)S(1)}, bf16[32,4,4096]{2,1,0:T(4,128)(2,1)}, u32[]{:S(2)}) copy-start(bf16[32,4,4096]{2,1,0:T(4,128)(2,1)} %param.9) | copy-start | bytes 3145732
  42.2 12.6 %copy-start.2 = (s32[32]{0:T(128)S(1)}, s32[32]{0:T(128)}, u32[]{:S(2)}) copy-start(s32[32]{0:T(128)} %param.12) | copy-start | bytes 388
  170.2 6.8 %copy-start = (f32[32,4,256,4,8]{2,4,3,1,0:T(8,128)S(1)}, f32[32,4,256,4,8]{2,4,3,1,0:T(8,128)}, u32[]{:S(2)}) copy-start(f32[32,4,256,4,8]{2,4,3,1,0:T(8,128)} %get-tuple-element.9) | copy-start | bytes 12582916
Sparse Core Ops, SparseCore 0:
  9.5 12.1 all-gather.2
  25.0 133.3 all-gather.4
where the time goes:
time: 197 us; the launch traced here: 195 us
  waiting for transfers between devices  91.7 us (47%)
  local copies, waits for them, and re-layouts  49 us (25%)
  matrix products  31.6 us (16%)
  between operations  14.9 us (8%)
  other arithmetic  7.88 us (4%)
    all_gather x1, waiting for transfers between devices, on_device(): weights_whole = lax.all_gather(weight_piece, 'rep', axis=0, tiled=True)  91 us
    reshape x1, local copies, waits for them, and re-layouts, on_device(): old_kv.reshape(feature_count, 2 * local_width)  17.8 us
    reshape x1, local copies, waits for them, and re-layouts, attend(): cached_keys = key_cache.reshape(row_count, context, head_count, depth)  12.6 us
    reshape x1, local copies, waits for them, and re-layouts, attend(): cached_values = value_cache.reshape(row_count, context, head_count, depth)  12.6 us
    dot_general x1, matrix products, attend(): jnp.einsum('rshgd,rthd->rshgt', grouped, cached_keys, preferred_element_t...  8.41 us
    dot_general x1, matrix products, attend(): jnp.einsum('rshgt,rthd->rshgd', cache_probs, cached_values, preferred_ele...  5.82 us
    dot_general x1, matrix products, on_device(): jnp.dot(flattened, old_kv.reshape(feature_count, 2 * local_width), prefer...  5.78 us
    dot_general x1, matrix products, on_device(): jnp.dot(flattened, weights_whole, preferred_element_type=jnp.float32)  5.78 us
  transfers between devices with their start and end apart: 2, of which 1 were waited for; matrix products, arithmetic and copies ran while one was open for 30% of the time, Pallas kernels for 0%

commit v1 on v0

v1 whole, which is shorter than its diff:
```python
import functools

import jax
import jax.numpy as jnp
from jax import lax
from jax.experimental import pallas as pl
from jax.experimental.pallas import tpu as pltpu
from jax.sharding import PartitionSpec as P

HEAD = 128
GROUP = 4
NEG = -1e30

epsilon = 1e-06


def cached_kernel(lengths, q_ref, k_ref, v_ref, *rest):
    qr_ref, acc_ref, stat_ref = rest[-3:]
    length = lengths[pl.program_id(0)]
    steps = q_ref.shape[1]
    context = k_ref.shape[1]
    heads = k_ref.shape[2] // HEAD
    per = q_ref.shape[2] // (heads * HEAD)
    scaling = HEAD ** (-0.5)
    visible = lax.broadcasted_iota(jnp.int32, (per * steps, context), 1) < length
    lane = lax.broadcasted_iota(jnp.int32, (per * steps, HEAD), 1)
    for h in range(heads):
        q = jnp.concatenate(
            [
                q_ref[0, :, (h * per + g) * HEAD : (h * per + g + 1) * HEAD].astype(jnp.float32)
                for g in range(per)
            ],
            axis=0,
        ).astype(jnp.bfloat16)
        qr_ref[0, h] = q
        cols = slice(h * HEAD, (h + 1) * HEAD)
        scores = (
            lax.dot_general(
                q, k_ref[0, :, cols], (((1,), (1,)), ((), ())), preferred_element_type=jnp.float32
            )
            * scaling
        )
        scores = jnp.where(visible, scores, NEG)
        highest = jnp.max(scores, axis=-1, keepdims=True)
        weights = jnp.where(visible, jnp.exp(scores - highest), 0.0)
        total = jnp.sum(weights, axis=-1, keepdims=True)
        acc_ref[0, h] = jnp.dot(
            weights.astype(jnp.bfloat16), v_ref[0, :, cols], preferred_element_type=jnp.float32
        )
        stat_ref[0, h] = jnp.where(lane < HEAD // 2, highest, total)


def cached_attention(queries, key_cache, value_cache, lengths, after):
    rows, steps, width = queries.shape
    context, local = key_cache.shape[1:]
    heads = local // HEAD
    count = width // (heads * HEAD) * steps
    block = lambda *shape: pl.BlockSpec((1,) + shape, lambda r, n: (r,) + (0,) * len(shape))
    piece = (rows, heads, count, HEAD)
    return pl.pallas_call(
        cached_kernel,
        grid_spec=pltpu.PrefetchScalarGridSpec(
            num_scalar_prefetch=1,
            grid=(rows,),
            in_specs=[block(steps, width), block(context, local), block(context, local)]
            + [pl.BlockSpec(memory_space=pl.ANY)] * len(after),
            out_specs=[block(heads, count, HEAD)] * 3,
        ),
        out_shape=(
            jax.ShapeDtypeStruct(piece, jnp.bfloat16),
            jax.ShapeDtypeStruct(piece, jnp.float32),
            jax.ShapeDtypeStruct(piece, jnp.float32),
        ),
        cost_estimate=pl.CostEstimate(
            flops=4 * rows * heads * count * context * HEAD,
            bytes_accessed=4 * rows * context * local + 14 * rows * heads * count * HEAD,
            transcendentals=rows * heads * count * context,
        ),
    )(lengths, queries, key_cache, value_cache, *after)


def final_kernel(adopt, qr_ref, acc_ref, stat_ref, sk, sv, ok, ov, rk, rv, out_ref, nk_ref, nv_ref):
    rows, _, count, _ = qr_ref.shape
    flat = sk.shape[0]
    steps = flat // rows
    step = lax.rem(lax.broadcasted_iota(jnp.int32, (flat, HEAD), 0), steps)
    fresh = step >= adopt[0]
    current_k = ok[...]
    current_v = ov[...]
    for d in range(rk.shape[0]):
        current_k = current_k + rk[d].astype(jnp.float32)
        current_v = current_v + rv[d].astype(jnp.float32)
    keys = jnp.where(fresh, current_k, sk[...])
    values = jnp.where(fresh, current_v, sv[...])
    keys = keys * lax.rsqrt(jnp.mean(keys * keys, axis=-1, keepdims=True) + epsilon)
    keys = keys.astype(jnp.bfloat16)
    values = values.astype(jnp.bfloat16)
    nk_ref[...] = keys
    nv_ref[...] = values
    every = rows * count
    q = qr_ref[...].reshape(every, HEAD)
    acc = acc_ref[...].reshape(every, HEAD)
    stat = stat_ref[...].reshape(every, HEAD)
    highest = stat[:, :1]
    total = stat[:, HEAD // 2 : HEAD // 2 + 1]
    scores = lax.dot_general(
        q, keys, (((1,), (1,)), ((), ())), preferred_element_type=jnp.float32
    ) * (HEAD ** (-0.5))
    i = lax.broadcasted_iota(jnp.int32, (every, flat), 0)
    j = lax.broadcasted_iota(jnp.int32, (every, flat), 1)
    visible = (i // count == j // steps) & (lax.rem(j, steps) <= lax.rem(i, steps))
    scores = jnp.where(visible, scores, NEG)
    top = jnp.maximum(highest, jnp.max(scores, axis=-1, keepdims=True))
    weights = jnp.where(visible, jnp.exp(scores - top), 0.0)
    decay = jnp.exp(highest - top)
    denominator = total * decay + jnp.sum(weights, axis=-1, keepdims=True)
    mixed = acc * decay + jnp.dot(
        weights.astype(jnp.bfloat16), values, preferred_element_type=jnp.float32
    )
    mixed = (mixed / denominator).reshape(rows, count, HEAD)
    for g in range(count // steps):
        out_ref[:, :, g * HEAD : (g + 1) * HEAD] = mixed[:, g * steps : (g + 1) * steps, :].astype(
            jnp.bfloat16
        )


def final_attention(adopt, qr, acc, stat, stale, own, received):
    rows, heads, count, _ = qr.shape
    flat, both = stale.shape
    steps = flat // rows
    piece = pl.BlockSpec((rows, 1, count, HEAD), lambda h, n: (0, h, 0, 0))
    key = pl.BlockSpec((flat, HEAD), lambda h, n: (0, h))
    value = pl.BlockSpec((flat, HEAD), lambda h, n: (0, heads + h))
    others = received.shape[0]
    rkey = pl.BlockSpec((others, flat, HEAD), lambda h, n: (0, 0, h))
    rvalue = pl.BlockSpec((others, flat, HEAD), lambda h, n: (0, 0, heads + h))
    per = count // steps
    return pl.pallas_call(
        final_kernel,
        grid_spec=pltpu.PrefetchScalarGridSpec(
            num_scalar_prefetch=1,
            grid=(heads,),
            in_specs=[piece] * 3 + [key, value, key, value, rkey, rvalue],
            out_specs=[
                pl.BlockSpec((rows, steps, per * HEAD), lambda h, n: (0, 0, h)),
                key,
                key,
            ],
        ),
        out_shape=(
            jax.ShapeDtypeStruct((rows, steps, heads * per * HEAD), jnp.bfloat16),
            jax.ShapeDtypeStruct((flat, both // 2), jnp.bfloat16),
            jax.ShapeDtypeStruct((flat, both // 2), jnp.bfloat16),
        ),
        compiler_params=pltpu.CompilerParams(vmem_limit_bytes=40 * 1024 * 1024),
        cost_estimate=pl.CostEstimate(
            flops=4 * rows * heads * count * flat * HEAD,
            bytes_accessed=12 * rows * heads * count * HEAD,
            transcendentals=rows * heads * count * flat,
        ),
    )(adopt, qr, acc, stat, stale, stale, own, own, received, received)


def on_device(replicas, parts, hidden, queries, key_cache, value_cache, lengths, adopt, old_kv, fresh_kv):
    outer = replicas // GROUP
    rows, steps, share = hidden.shape
    width = share * parts
    flat = rows * steps
    both = 2 * old_kv.shape[2]
    plane = lax.axis_index("rep") // GROUP

    piece = fresh_kv.reshape(fresh_kv.shape[0], both)
    groups = [[z * GROUP + p for p in range(GROUP)] for z in range(outer)]
    weights = lax.all_gather(piece, "rep", axis=0, tiled=True, axis_index_groups=groups)

    mine = hidden.reshape(flat, share)
    me = lax.axis_index("tp")
    whole = jnp.zeros((flat, width), jnp.bfloat16)
    whole = lax.dynamic_update_slice(whole, mine, (0, me * share))
    for d in range(1, parts):
        got = lax.ppermute(mine, "tp", [(t, (t + d) % parts) for t in range(parts)])
        whole = lax.dynamic_update_slice(whole, got, (0, lax.rem(me - d + parts, parts) * share))
    widened = whole.astype(jnp.float32)
    normed = (
        widened * lax.rsqrt(jnp.mean(widened * widened, axis=-1, keepdims=True) + epsilon)
    ).astype(jnp.bfloat16)

    depth = width // outer

    def shift(d):
        return [
            (z * GROUP + p, (z + d) % outer * GROUP + p) for z in range(outer) for p in range(GROUP)
        ]

    def columns(z):
        return lax.dynamic_slice(normed, (0, z * depth), (flat, depth))

    inputs = [columns(plane)]
    for d in range(1, outer):
        inputs.append(lax.ppermute(columns(lax.rem(plane + d, outer)), "rep", shift(d)))
    own = jnp.dot(inputs[0], weights, preferred_element_type=jnp.float32)
    received = []
    sent = []
    for d in range(1, outer):
        partial = jnp.dot(inputs[d], weights, preferred_element_type=jnp.float32)
        sent.append(partial.astype(jnp.bfloat16))
        received.append(lax.ppermute(sent[-1], "rep", shift(outer - d)))
    received = jnp.stack(received)

    old_kv, _ = lax.optimization_barrier((old_kv, normed[:1, :1]))
    stale = jnp.dot(normed, old_kv.reshape(width, both), preferred_element_type=jnp.float32)
    qr, acc, stat = cached_attention(queries, key_cache, value_cache, lengths, sent)
    attended, keys, values = final_attention(adopt, qr, acc, stat, stale, own, received)
    appended = jnp.stack([keys, values], axis=1).reshape(rows, steps, 2, both // 2)
    return attended, appended


def solution(mesh):
    placed = (
        P("rep", None, "tp"),
        P("rep", None, "tp"),
        P("rep", None, "tp"),
        P("rep", None, "tp"),
        P("rep"),
        P("rep"),
        P(None, None, "tp"),
        P("rep", None, "tp"),
    )
    return jax.shard_map(
        functools.partial(on_device, mesh.shape["rep"], mesh.shape["tp"]),
        mesh=mesh,
        in_specs=placed,
        out_specs=(P("rep", None, "tp"), P("rep", None, None, "tp")),
        check_vma=False,
    )
```

time: 197 us -> 125 us (0.63)
  waiting for transfers between devices: 91.7 us -> 15.3 us
  Pallas kernels: 0 us -> 45.6 us
  local copies, waits for them, and re-layouts: 49 us -> 17.7 us
  matrix products: 31.6 us -> 14.1 us
  starting transfers between devices: 0.08 us -> 13.3 us
  other arithmetic: 7.88 us -> 3.16 us
    all_gather x2 -> x1, waiting for transfers between devices: 91 us -> 14 us  [on_device(): lax.all_gather(piece, 'rep', axis=0, tiled=True, axis_index_groups=groups)]
    pallas_call x0 -> x2, Pallas kernels: none -> 45.6 us  [the longest x1 37.2 us: cached_attention(): pl.pallas_call(cached_kernel, grid_spec=pltpu.PrefetchScalarGridSpec(num_...]
    reshape x5 -> x1, local copies, waits for them, and re-layouts: 44.4 us -> 1.5 us  [on_device(): mine = hidden.reshape(flat, share)]
    dot_general x6 -> x5, matrix products: 31.6 us -> 14.1 us  [the longest x3 6.9 us: on_device(): partial = jnp.dot(inputs[d], weights, preferred_element_type=jnp.float32)]
    ppermute x0 -> x7, starting transfers between devices: none -> 13.3 us  [the longest x3 6.44 us: on_device(): lax.ppermute(columns(lax.rem(plane + d, outer)), 'rep', shift(d))]
    unnamed x11 -> x14, local copies, waits for them, and re-layouts: 4.42 us -> 14.7 us
    reduce_sum x3 -> x0, other arithmetic: 3.19 us -> none  [the longest x1 1.78 us: attend(): jnp.sum(cache_weights, axis=-1, keepdims=True)]
    another operation x1 -> x2, other arithmetic: 0.03 us -> 2.5 us  [the longest x1 1.3 us: on_device(): jnp.stack([keys, values], axis=1).reshape(rows, steps, 2, both // 2)]
  transfers between devices with their start and end apart: 2 -> 8, of which waited for: 1 -> 2; matrix products, arithmetic and copies ran while one was open for 30% -> 23% of each run, Pallas kernels for 0% -> 30%
where the time goes in v1:
time: 125 us; the launch traced here: 124 us
  Pallas kernels  45.6 us (36%)
  local copies, waits for them, and re-layouts  17.7 us (14%)
  waiting for transfers between devices  15.3 us (12%)
  between operations  14.9 us (12%)
  matrix products  14.1 us (11%)
  starting transfers between devices  13.3 us (11%)
  other arithmetic  3.16 us (3%)
    pallas_call x1, Pallas kernels, cached_attention(): pl.pallas_call(cached_kernel, grid_spec=pltpu.PrefetchScalarGridSpec(num_...  37.2 us
    unnamed x14, local copies, waits for them, and re-layouts  14.7 us
    all_gather x1, waiting for transfers between devices, on_device(): lax.all_gather(piece, 'rep', axis=0, tiled=True, axis_index_groups=groups)  14 us
    pallas_call x1, Pallas kernels, final_attention(): pl.pallas_call(final_kernel, grid_spec=pltpu.PrefetchScalarGridSpec(num_s...  8.42 us
    dot_general x3, matrix products, on_device(): partial = jnp.dot(inputs[d], weights, preferred_element_type=jnp.float32)  6.9 us
    ppermute x3, starting transfers between devices, on_device(): lax.ppermute(columns(lax.rem(plane + d, outer)), 'rep', shift(d))  6.44 us
    ppermute x3, starting transfers between devices, on_device(): received.append(lax.ppermute(sent[-1], 'rep', shift(outer - d)))  6.35 us
    dot_general x1, matrix products, on_device(): jnp.dot(normed, old_kv.reshape(width, both), preferred_element_type=jnp.f...  5.59 us
  transfers between devices with their start and end apart: 8, of which 2 were waited for; matrix products, arithmetic and copies ran while one was open for 23% of the time, Pallas kernels for 30%

profile of v1, /device:TPU:0, one launch (start us, length us, event | category | flops | bytes accessed | tf_op | source)
XLA Modules:
  0.0 124.1 jit_solution(9990219431293516060)
XLA Ops:
  7.2 0.0 all-gather.2.cloned.1.call-start
  7.2 2.0 %copy.12 = bf16[40,8,2,512]{3,1,2,0:T(8,128)(2,1)} copy(bf16[40,8,2,512]{3,2,1,0:T(2,128)(2,1)} %bitcast.19) | data formatting | bytes 1310720
  9.2 0.0 all-gather.2.cloned.1.call-update
  9.3 1.5 %reshape.26 = bf16[128,2560]{1,0:T(8,128)(2,1)S(1)} reshape(bf16[32,4,2560]{2,1,0:T(4,128)(2,1)} %param.8) | data formatting | bytes 1310720 | tf_op jit(solution)/shard_map/reshape | solution.py:176
  10.8 0.5 collective-permute-start
  11.3 11.5 %copy.13 = bf16[640,8,2,512]{3,1,2,0:T(8,128)(2,1)} copy(bf16[640,8,2,512]{3,2,1,0:T(2,128)(2,1)} %bitcast.17) | data formatting | bytes 20971520
  23.4 0.1 broadcast_in_dim.4
  23.6 0.1 constant_dynamic-update-slice_fusion.1
  23.6 0.1 constant_dynamic-update-slice_fusion
  23.7 0.3 fusion
  24.1 0.3 fusion.1
  24.4 1.1 constant_dynamic-slice_fusion
  25.5 2.5 %collective-permute-start.1 = (bf16[128,1280]{1,0:T(8,128)(2,1)S(1)}, bf16[128,1280]{1,0:T(8,128)(2,1)}, u32[]{:S(2)}, u32[]{:S(2)}) collective-permute-start(bf16[128,1280]{1,0:T(8,128)(2,1)S(1)} %get-tuple-element.16), channel_id=1, source_target_pairs={{0,8},{2,10},{4,12},{6,14},{8,16},{10,18},{12,20},{14,22},{16,24},... | collective-permute-start | bytes 983048 | tf_op jit(solution)/shard_map/ppermute | solution.py:200
  28.0 2.6 %collective-permute-start.2 = (bf16[128,1280]{1,0:T(8,128)(2,1)}, bf16[128,1280]{1,0:T(8,128)(2,1)}, u32[]{:S(2)}, u32[]{:S(2)}) collective-permute-start(bf16[128,1280]{1,0:T(8,128)(2,1)} %get-tuple-element.15), channel_id=1, source_target_pairs={{0,16},{2,18},{4,20},{6,22},{8,24},{10,26},{12,28},{14,30},{16,0},... | collective-permute-start | bytes 983048 | tf_op jit(solution)/shard_map/ppermute | solution.py:200
  30.6 1.3 %collective-permute-start.3 = (bf16[128,1280]{1,0:T(8,128)(2,1)}, bf16[128,1280]{1,0:T(8,128)(2,1)}, u32[]{:S(2)}, u32[]{:S(2)}) collective-permute-start(bf16[128,1280]{1,0:T(8,128)(2,1)} %get-tuple-element.14), channel_id=1, source_target_pairs={{0,24},{2,26},{4,28},{6,30},{8,0},{10,2},{12,4},{14,6},{16,8},{18,... | collective-permute-start | bytes 983048 | tf_op jit(solution)/shard_map/ppermute | solution.py:200
  31.9 5.6 %fusion.5.sk.sv = f32[128,1024]{1,0:T(8,128)S(1)} fusion(bf16[128,5120]{1,0:T(8,128)(2,1)S(1)} %fusion.1, bf16[5120,1024]{1,0:T(8,128)(2,1)} %bitcast.16), kind=kOutput, calls=%fused_computation.18 | convolution fusion | flops 1342177280 | bytes 12320768 | tf_op jit(solution)/shard_map/dot_general | solution.py:211
  37.5 1.3 %collective-permute-done.1 = bf16[128,1280]{1,0:T(8,128)(2,1)} collective-permute-done((bf16[128,1280]{1,0:T(8,128)(2,1)S(1)}, bf16[128,1280]{1,0:T(8,128)(2,1)}, u32[]{:S(2)}, u32[]{:S(2)}) %collective-permute-start.1) | collective-permute-done | bytes 327712 | tf_op jit(solution)/shard_map/ppermute | solution.py:200
  38.8 14.0 %all-gather.2.cloned.1.call-done = bf16[1280,1024]{1,0:T(8,128)(2,1)} async-done(((bf16[320,1024]{1,0:T(8,128)(2,1)}), bf16[1280,1024]{1,0:T(8,128)(2,1)}) %all-gather.2.cloned.1.call-update) | async-done | bytes 2621456 | tf_op jit(solution)/shard_map/all_gather | solution.py:174
  52.8 2.5 %convolution_convert_fusion.2.rest_0_ = bf16[128,1024]{1,0:T(8,128)(2,1)S(1)} fusion(bf16[128,1280]{1,0:T(8,128)(2,1)} %collective-permute-done.1, bf16[1280,1024]{1,0:T(8,128)(2,1)} %all-gather.2.cloned.1.call-done), kind=kOutput, calls=%fused_computation.6 | convolution fusion | flops 335675392 | bytes 3211264 | tf_op jit(solution)/shard_map/dot_general | solution.py:205
  55.3 0.0 copy-start.5
  55.3 3.4 %collective-permute-start.4 = (bf16[128,1024]{1,0:T(8,128)(2,1)S(1)}, bf16[128,1024]{1,0:T(8,128)(2,1)}, u32[]{:S(2)}, u32[]{:S(2)}) collective-permute-start(bf16[128,1024]{1,0:T(8,128)(2,1)S(1)} %convolution_convert_fusion.2.rest_0_), channel_id=1, source_target_pairs={{0,24},{2,26},{4,28},{6,30},{8,0},{10,2},{12,4},{14,6},{16,8},{18,... | collective-permute-start | bytes 786440 | tf_op jit(solution)/shard_map/ppermute | solution.py:207
  58.7 2.2 %convolution_convert_fusion.1.rest_1_ = bf16[128,1024]{1,0:T(8,128)(2,1)} fusion(bf16[128,1280]{1,0:T(8,128)(2,1)} %collective-permute-done.2, bf16[1280,1024]{1,0:T(8,128)(2,1)S(1)} %copy-done.3), kind=kOutput, calls=%fused_computation.5 | convolution fusion | flops 335675392 | bytes 3211264 | tf_op jit(solution)/shard_map/dot_general | solution.py:205
  60.9 2.2 %convolution_convert_fusion.rest_2_ = bf16[128,1024]{1,0:T(8,128)(2,1)} fusion(bf16[128,1280]{1,0:T(8,128)(2,1)} %collective-permute-done.3, bf16[1280,1024]{1,0:T(8,128)(2,1)S(1)} %copy-done.3), kind=kOutput, calls=%fused_computation.4 | convolution fusion | flops 335675392 | bytes 3211264 | tf_op jit(solution)/shard_map/dot_general | solution.py:205
  63.1 3.0 %collective-permute-start.6 = (bf16[128,1024]{1,0:T(8,128)(2,1)}, bf16[128,1024]{1,0:T(8,128)(2,1)}, u32[]{:S(2)}, u32[]{:S(2)}) collective-permute-start(bf16[128,1024]{1,0:T(8,128)(2,1)} %convolution_convert_fusion.rest_2_), channel_id=1, source_target_pairs={{0,8},{2,10},{4,12},{6,14},{8,16},{10,18},{12,20},{14,22},{16,24},... | collective-permute-start | bytes 786440 | tf_op jit(solution)/shard_map/ppermute | solution.py:207
  66.1 37.2 %shard_map.95 = (bf16[32,4,32,128]{3,2,1,0:T(8,128)(2,1)}, f32[32,4,32,128]{3,2,1,0:T(8,128)}, f32[32,4,32,128]{3,2,1,0:T(8,128)}) custom-call(s32[32]{0:T(128)} %lengths.1, bf16[32,4,4096]{2,1,0:T(4,128)(2,1)} %q_ref.1, bf16[32,256,512]{2,1,0:T(8,128)(2,1)} %k_ref.1, bf16[32,256,512]{2,1,0:T(8,128)(2,1)} %v_ref.1, bf16[128,1024]{1,0:T(8,128)(2,1)} %copy-done.5, ...), custom_call_target="tpu_custom_call" | custom-call | flops 536870912 | bytes 24117248 | tf_op jit(solution)/shard_map/pallas_call | solution.py:60
  103.2 1.6 %fusion.2.ok.ov = f32[128,1024]{1,0:T(8,128)S(1)} fusion(bf16[1280,1024]{1,0:T(8,128)(2,1)S(1)} %copy-done.3, bf16[128,5120]{1,0:T(8,128)(2,1)} %copy-done.4, s32[]{:T(128)S(6)} %select_n.29), kind=kOutput, calls=%fused_computation.8 | convolution fusion | flops 335544320 | bytes 3473412 | tf_op jit(solution)/shard_map/dot_general | solution.py:201
  104.9 1.2 pad_maximum_fusion.rk.rv
  106.1 1.2 copy-done.2
  107.4 8.4 %shard_map.96 = (bf16[32,4,4096]{2,1,0:T(4,128)(2,1)}, bf16[128,512]{1,0:T(8,128)(2,1)S(1)}, bf16[128,512]{1,0:T(8,128)(2,1)S(1)}) custom-call(s32[1]{0:T(128)S(6)} %copy.16.adopt, bf16[32,4,32,128]{3,2,1,0:T(8,128)(2,1)S(1)} %copy-done.2, f32[32,4,32,128]{3,2,1,0:T(8,128)S(1)} %copy-done, f32[32,4,32,128]{3,2,1,0:T(8,128)S(1)} %copy-done.1, ...), custom_call_target="tpu_custom_call" | custom-call | flops 268435456 | bytes 6291456 | tf_op jit(solution)/shard_map/pallas_call | solution.py:138
  115.8 0.1 stack.28
  115.8 0.1 stack.29
  115.9 1.3 %pad_maximum_fusion.1 = bf16[32,4,2,512]{3,2,1,0:T(2,128)(2,1)} fusion(bf16[32,4,1,512]{3,2,1,0:T(2,128)(2,1)S(1)} %stack.29, bf16[32,4,1,512]{3,2,1,0:T(2,128)(2,1)S(1)} %stack.28), kind=kLoop, calls=%fused_computation.10 | loop fusion | flops 524288 | bytes 524288 | tf_op jit(solution)/shard_map/stack | solution.py:214
  (18 shorter events, 0.0 us)
Async XLA Ops:
  7.2 45.6 %all-gather.2.cloned.1.call-start = ((), (), s32[]{:S(2)}) async-start(), calls=%async_computation | async-start | bytes 3276800 | tf_op jit(solution)/shard_map/all_gather | solution.py:174
  10.8 12.9 %collective-permute-start = (bf16[128,2560]{1,0:T(8,128)(2,1)S(1)}, bf16[128,2560]{1,0:T(8,128)(2,1)S(1)}, u32[]{:S(2)}, u32[]{:S(2)}) collective-permute-start(bf16[128,2560]{1,0:T(8,128)(2,1)S(1)} %reshape.26), channel_id=1, source_target_pairs={{0,1},{1,0},{2,3},{3,2},{4,5},{5,4},{6,7},{7,6},{8,9},{9,8},{10,11... | collective-permute-start | bytes 1966088 | tf_op jit(solution)/shard_map/ppermute | solution.py:181
  24.4 13.1 %copy-start.4 = (bf16[128,5120]{1,0:T(8,128)(2,1)}, bf16[128,5120]{1,0:T(8,128)(2,1)S(1)}, u32[]{:S(2)}) copy-start(bf16[128,5120]{1,0:T(8,128)(2,1)S(1)} %fusion.1) | copy-start | bytes 3932164
  25.5 13.3 %collective-permute-start.1 = (bf16[128,1280]{1,0:T(8,128)(2,1)S(1)}, bf16[128,1280]{1,0:T(8,128)(2,1)}, u32[]{:S(2)}, u32[]{:S(2)}) collective-permute-start(bf16[128,1280]{1,0:T(8,128)(2,1)S(1)} %get-tuple-element.16), channel_id=1, source_target_pairs={{0,8},{2,10},{4,12},{6,14},{8,16},{10,18},{12,20},{14,22},{16,24},... | collective-permute-start | bytes 983048 | tf_op jit(solution)/shard_map/ppermute | solution.py:200
  28.0 30.7 %collective-permute-start.2 = (bf16[128,1280]{1,0:T(8,128)(2,1)}, bf16[128,1280]{1,0:T(8,128)(2,1)}, u32[]{:S(2)}, u32[]{:S(2)}) collective-permute-start(bf16[128,1280]{1,0:T(8,128)(2,1)} %get-tuple-element.15), channel_id=1, source_target_pairs={{0,16},{2,18},{4,20},{6,22},{8,24},{10,26},{12,28},{14,30},{16,0},... | collective-permute-start | bytes 983048 | tf_op jit(solution)/shard_map/ppermute | solution.py:200
  30.6 30.4 %collective-permute-start.3 = (bf16[128,1280]{1,0:T(8,128)(2,1)}, bf16[128,1280]{1,0:T(8,128)(2,1)}, u32[]{:S(2)}, u32[]{:S(2)}) collective-permute-start(bf16[128,1280]{1,0:T(8,128)(2,1)} %get-tuple-element.14), channel_id=1, source_target_pairs={{0,24},{2,26},{4,28},{6,30},{8,0},{10,2},{12,4},{14,6},{16,8},{18,... | collective-permute-start | bytes 983048 | tf_op jit(solution)/shard_map/ppermute | solution.py:200
  52.8 5.9 %copy-start.3 = (bf16[1280,1024]{1,0:T(8,128)(2,1)S(1)}, bf16[1280,1024]{1,0:T(8,128)(2,1)}, u32[]{:S(2)}) copy-start(bf16[1280,1024]{1,0:T(8,128)(2,1)} %all-gather.2.cloned.1.call-done) | copy-start | bytes 7864324
  55.3 7.8 %copy-start.5 = (bf16[128,1024]{1,0:T(8,128)(2,1)}, bf16[128,1024]{1,0:T(8,128)(2,1)S(1)}, u32[]{:S(2)}) copy-start(bf16[128,1024]{1,0:T(8,128)(2,1)S(1)} %convolution_convert_fusion.2.rest_0_) | copy-start | bytes 786436
  55.3 49.6 %collective-permute-start.4 = (bf16[128,1024]{1,0:T(8,128)(2,1)S(1)}, bf16[128,1024]{1,0:T(8,128)(2,1)}, u32[]{:S(2)}, u32[]{:S(2)}) collective-permute-start(bf16[128,1024]{1,0:T(8,128)(2,1)S(1)} %convolution_convert_fusion.2.rest_0_), channel_id=1, source_target_pairs={{0,24},{2,26},{4,28},{6,30},{8,0},{10,2},{12,4},{14,6},{16,8},{18,... | collective-permute-start | bytes 786440 | tf_op jit(solution)/shard_map/ppermute | solution.py:207
  60.9 44.0 %collective-permute-start.5 = (bf16[128,1024]{1,0:T(8,128)(2,1)}, bf16[128,1024]{1,0:T(8,128)(2,1)}, u32[]{:S(2)}, u32[]{:S(2)}) collective-permute-start(bf16[128,1024]{1,0:T(8,128)(2,1)} %convolution_convert_fusion.1.rest_1_), channel_id=1, source_target_pairs={{0,16},{2,18},{4,20},{6,22},{8,24},{10,26},{12,28},{14,30},{16,0},... | collective-permute-start | bytes 786440 | tf_op jit(solution)/shard_map/ppermute | solution.py:207
  63.1 41.8 %collective-permute-start.6 = (bf16[128,1024]{1,0:T(8,128)(2,1)}, bf16[128,1024]{1,0:T(8,128)(2,1)}, u32[]{:S(2)}, u32[]{:S(2)}) collective-permute-start(bf16[128,1024]{1,0:T(8,128)(2,1)} %convolution_convert_fusion.rest_2_), channel_id=1, source_target_pairs={{0,8},{2,10},{4,12},{6,14},{8,16},{10,18},{12,20},{14,22},{16,24},... | collective-permute-start | bytes 786440 | tf_op jit(solution)/shard_map/ppermute | solution.py:207
  103.2 2.9 %copy-start = (f32[32,4,32,128]{3,2,1,0:T(8,128)S(1)}, f32[32,4,32,128]{3,2,1,0:T(8,128)}, u32[]{:S(2)}) copy-start(f32[32,4,32,128]{3,2,1,0:T(8,128)} %get-tuple-element.9.acc_ref) | copy-start | bytes 6291460
  103.2 2.9 %copy-start.1 = (f32[32,4,32,128]{3,2,1,0:T(8,128)S(1)}, f32[32,4,32,128]{3,2,1,0:T(8,128)}, u32[]{:S(2)}) copy-start(f32[32,4,32,128]{3,2,1,0:T(8,128)} %get-tuple-element.10.stat_ref) | copy-start | bytes 6291460
  106.1 1.2 copy-start.2
Sparse Core Ops, SparseCore 0:
  10.4 42.3 all-gather.1

commit v2 on v1

--- a/solution.py
+++ b/solution.py
@@ -1,4 +1,5 @@
 import functools
+import math
 
 import jax
 import jax.numpy as jnp
@@ -10,44 +11,41 @@
 HEAD = 128
 GROUP = 4
 NEG = -1e30
+TO_EXP2 = HEAD ** (-0.5) * math.log2(math.e)
 
 epsilon = 1e-06
 
 
 def cached_kernel(lengths, q_ref, k_ref, v_ref, *rest):
     qr_ref, acc_ref, stat_ref = rest[-3:]
-    length = lengths[pl.program_id(0)]
-    steps = q_ref.shape[1]
+    rows, steps = q_ref.shape[:2]
     context = k_ref.shape[1]
     heads = k_ref.shape[2] // HEAD
     per = q_ref.shape[2] // (heads * HEAD)
-    scaling = HEAD ** (-0.5)
-    visible = lax.broadcasted_iota(jnp.int32, (per * steps, context), 1) < length
+    first = pl.program_id(0) * rows
+    position = lax.broadcasted_iota(jnp.int32, (per * steps, context), 1)
     lane = lax.broadcasted_iota(jnp.int32, (per * steps, HEAD), 1)
-    for h in range(heads):
-        q = jnp.concatenate(
-            [
-                q_ref[0, :, (h * per + g) * HEAD : (h * per + g + 1) * HEAD].astype(jnp.float32)
-                for g in range(per)
-            ],
-            axis=0,
-        ).astype(jnp.bfloat16)
-        qr_ref[0, h] = q
-        cols = slice(h * HEAD, (h + 1) * HEAD)
-        scores = (
-            lax.dot_general(
-                q, k_ref[0, :, cols], (((1,), (1,)), ((), ())), preferred_element_type=jnp.float32
+    for r in range(rows):
+        visible = position < lengths[first + r]
+        wide = q_ref[r].astype(jnp.float32)
+        for h in range(heads):
+            q = jnp.concatenate(
+                [wide[:, (h * per + g) * HEAD : (h * per + g + 1) * HEAD] for g in range(per)],
+                axis=0,
+            ).astype(jnp.bfloat16)
+            qr_ref[r, h] = q
+            cols = slice(h * HEAD, (h + 1) * HEAD)
+            scores = lax.dot_general(
+                q, k_ref[r, :, cols], (((1,), (1,)), ((), ())), preferred_element_type=jnp.float32
             )
-            * scaling
-        )
-        scores = jnp.where(visible, scores, NEG)
-        highest = jnp.max(scores, axis=-1, keepdims=True)
-        weights = jnp.where(visible, jnp.exp(scores - highest), 0.0)
-        total = jnp.sum(weights, axis=-1, keepdims=True)
-        acc_ref[0, h] = jnp.dot(
-            weights.astype(jnp.bfloat16), v_ref[0, :, cols], preferred_element_type=jnp.float32
-        )
-        stat_ref[0, h] = jnp.where(lane < HEAD // 2, highest, total)
+            scores = jnp.where(visible, scores, NEG)
+            highest = jnp.max(scores, axis=-1, keepdims=True)
+            weights = jnp.exp2((scores - highest) * TO_EXP2)
+            total = jnp.sum(weights, axis=-1, keepdims=True)
+            acc_ref[r, h] = jnp.dot(
+                weights.astype(jnp.bfloat16), v_ref[r, :, cols], preferred_element_type=jnp.float32
+            )
+            stat_ref[r, h] = jnp.where(lane < HEAD // 2, highest, total)
 
 
 def cached_attention(queries, key_cache, value_cache, lengths, after):
@@ -55,13 +53,14 @@
     context, local = key_cache.shape[1:]
     heads = local // HEAD
     count = width // (heads * HEAD) * steps
-    block = lambda *shape: pl.BlockSpec((1,) + shape, lambda r, n: (r,) + (0,) * len(shape))
+    some = 4 if rows % 4 == 0 else 1
+    block = lambda *shape: pl.BlockSpec((some,) + shape, lambda r, n: (r,) + (0,) * len(shape))
     piece = (rows, heads, count, HEAD)
     return pl.pallas_call(
         cached_kernel,
         grid_spec=pltpu.PrefetchScalarGridSpec(
             num_scalar_prefetch=1,
-            grid=(rows,),
+            grid=(rows // some,),
             in_specs=[block(steps, width), block(context, local), block(context, local)]
             + [pl.BlockSpec(memory_space=pl.ANY)] * len(after),
             out_specs=[block(heads, count, HEAD)] * 3,
@@ -71,6 +70,7 @@
             jax.ShapeDtypeStruct(piece, jnp.float32),
             jax.ShapeDtypeStruct(piece, jnp.float32),
         ),
+        compiler_params=pltpu.CompilerParams(vmem_limit_bytes=32 * 1024 * 1024),
         cost_estimate=pl.CostEstimate(
             flops=4 * rows * heads * count * context * HEAD,
             bytes_accessed=4 * rows * context * local + 14 * rows * heads * count * HEAD,
@@ -79,7 +79,9 @@
     )(lengths, queries, key_cache, value_cache, *after)
 
 
-def final_kernel(adopt, qr_ref, acc_ref, stat_ref, sk, sv, ok, ov, rk, rv, out_ref, nk_ref, nv_ref):
+def final_kernel(adopt, qr_ref, acc_ref, stat_ref, sk, sv, ok, ov, *rest):
+    out_ref, nk_ref, nv_ref = rest[-3:]
+    received = rest[:-3]
     rows, _, count, _ = qr_ref.shape
     flat = sk.shape[0]
     steps = flat // rows
@@ -87,9 +89,9 @@
     fresh = step >= adopt[0]
     current_k = ok[...]
     current_v = ov[...]
-    for d in range(rk.shape[0]):
-        current_k = current_k + rk[d].astype(jnp.float32)
-        current_v = current_v + rv[d].astype(jnp.float32)
+    for d in range(len(received) // 2):
+        current_k = current_k + received[2 * d][...].astype(jnp.float32)
+        current_v = current_v + received[2 * d + 1][...].astype(jnp.float32)
     keys = jnp.where(fresh, current_k, sk[...])
     values = jnp.where(fresh, current_v, sv[...])
     keys = keys * lax.rsqrt(jnp.mean(keys * keys, axis=-1, keepdims=True) + epsilon)
@@ -105,19 +107,20 @@
     total = stat[:, HEAD // 2 : HEAD // 2 + 1]
     scores = lax.dot_general(
         q, keys, (((1,), (1,)), ((), ())), preferred_element_type=jnp.float32
-    ) * (HEAD ** (-0.5))
+    )
     i = lax.broadcasted_iota(jnp.int32, (every, flat), 0)
     j = lax.broadcasted_iota(jnp.int32, (every, flat), 1)
-    visible = (i // count == j // steps) & (lax.rem(j, steps) <= lax.rem(i, steps))
+    since = j - lax.shift_right_logical(i, count.bit_length() - 1) * steps
+    visible = (since >= 0) & (since <= (i & (steps - 1)))
     scores = jnp.where(visible, scores, NEG)
     top = jnp.maximum(highest, jnp.max(scores, axis=-1, keepdims=True))
-    weights = jnp.where(visible, jnp.exp(scores - top), 0.0)
-    decay = jnp.exp(highest - top)
+    weights = jnp.exp2((scores - top) * TO_EXP2)
+    decay = jnp.exp2((highest - top) * TO_EXP2)
     denominator = total * decay + jnp.sum(weights, axis=-1, keepdims=True)
     mixed = acc * decay + jnp.dot(
         weights.astype(jnp.bfloat16), values, preferred_element_type=jnp.float32
     )
-    mixed = (mixed / denominator).reshape(rows, count, HEAD)
+    mixed = (mixed * (1.0 / denominator)).reshape(rows, count, HEAD)
     for g in range(count // steps):
         out_ref[:, :, g * HEAD : (g + 1) * HEAD] = mixed[:, g * steps : (g + 1) * steps, :].astype(
             jnp.bfloat16
@@ -131,16 +134,14 @@
     piece = pl.BlockSpec((rows, 1, count, HEAD), lambda h, n: (0, h, 0, 0))
     key = pl.BlockSpec((flat, HEAD), lambda h, n: (0, h))
     value = pl.BlockSpec((flat, HEAD), lambda h, n: (0, heads + h))
-    others = received.shape[0]
-    rkey = pl.BlockSpec((others, flat, HEAD), lambda h, n: (0, 0, h))
-    rvalue = pl.BlockSpec((others, flat, HEAD), lambda h, n: (0, 0, heads + h))
+    doubled = [array for array in received for _ in range(2)]
     per = count // steps
     return pl.pallas_call(
         final_kernel,
         grid_spec=pltpu.PrefetchScalarGridSpec(
             num_scalar_prefetch=1,
             grid=(heads,),
-            in_specs=[piece] * 3 + [key, value, key, value, rkey, rvalue],
+            in_specs=[piece] * 3 + [key, value] * (2 + len(received)),
             out_specs=[
                 pl.BlockSpec((rows, steps, per * HEAD), lambda h, n: (0, 0, h)),
                 key,
@@ -158,7 +159,7 @@
             bytes_accessed=12 * rows * heads * count * HEAD,
             transcendentals=rows * heads * count * flat,
         ),
-    )(adopt, qr, acc, stat, stale, stale, own, own, received, received)
+    )(adopt, qr, acc, stat, stale, stale, own, own, *doubled)
 
 
 def on_device(replicas, parts, hidden, queries, key_cache, value_cache, lengths, adopt, old_kv, fresh_kv):
@@ -170,8 +171,13 @@
     plane = lax.axis_index("rep") // GROUP
 
     piece = fresh_kv.reshape(fresh_kv.shape[0], both)
-    groups = [[z * GROUP + p for p in range(GROUP)] for z in range(outer)]
-    weights = lax.all_gather(piece, "rep", axis=0, tiled=True, axis_index_groups=groups)
+    count = fresh_kv.shape[0]
+    spot = lax.axis_index("rep") % GROUP
+    weights = jnp.zeros((GROUP * count, both), jnp.bfloat16)
+    weights = lax.dynamic_update_slice(weights, piece, (spot * count, 0))
+    for k in range(1, GROUP):
+        got = lax.ppermute(piece, "rep", [(r, r ^ k) for r in range(replicas)])
+        weights = lax.dynamic_update_slice(weights, got, ((spot ^ k) * count, 0))
 
     mine = hidden.reshape(flat, share)
     me = lax.axis_index("tp")
@@ -205,7 +211,6 @@
         partial = jnp.dot(inputs[d], weights, preferred_element_type=jnp.float32)
         sent.append(partial.astype(jnp.bfloat16))
         received.append(lax.ppermute(sent[-1], "rep", shift(outer - d)))
-    received = jnp.stack(received)
 
     old_kv, _ = lax.optimization_barrier((old_kv, normed[:1, :1]))
     stale = jnp.dot(normed, old_kv.reshape(width, both), preferred_element_type=jnp.float32)

time: 125 us -> 108 us (0.86)
  starting transfers between devices: 13.3 us -> 30.6 us
  between operations: 14.9 us -> 1.64 us
  matrix products: 14.1 us -> 3.59 us
  Pallas kernels: 45.6 us -> 41.3 us
  waiting for transfers between devices: 15.3 us -> 12.4 us
  local copies, waits for them, and re-layouts: 17.7 us -> 16.3 us
    ppermute x3, starting transfers between devices: 6.35 us -> 20.8 us  [on_device(): received.append(lax.ppermute(sent[-1], 'rep', shift(outer - d)))]
    all_gather x1 -> x0, waiting for transfers between devices: 14 us -> none  [on_device(): lax.all_gather(piece, 'rep', axis=0, tiled=True, axis_index_groups=groups)]
    ppermute x0 -> x3, waiting for transfers between devices: none -> 7.8 us  [on_device(): got = lax.ppermute(piece, 'rep', [(r, r ^ k) for r in range(replicas)])]
    dot_general x3, matrix products: 6.9 us -> 1.55 us  [on_device(): partial = jnp.dot(inputs[d], weights, preferred_element_type=jnp.float32)]
    pallas_call x1, Pallas kernels: 37.2 us -> 32.8 us  [cached_attention(): pl.pallas_call(cached_kernel, grid_spec=pltpu.PrefetchScalarGridSpec(num_...]
    ppermute x0 -> x3, starting transfers between devices: none -> 4.11 us  [on_device(): got = lax.ppermute(piece, 'rep', [(r, r ^ k) for r in range(replicas)])]
    dot_general x1, matrix products: 5.59 us -> 1.52 us  [on_device(): jnp.dot(normed, old_kv.reshape(width, both), preferred_element_type=jnp.f...]
    ppermute x3, waiting for transfers between devices: 1.29 us -> 4.54 us  [on_device(): lax.ppermute(columns(lax.rem(plane + d, outer)), 'rep', shift(d))]
  transfers between devices with their start and end apart: 8 -> 10, of which waited for: 2 -> 2; matrix products, arithmetic and copies ran while one was open for 23% -> 18% of each run, Pallas kernels for 30% -> 30%
where the time goes in v2:
time: 108 us
  Pallas kernels  41.3 us (38%)
  starting transfers between devices  30.6 us (28%)
  local copies, waits for them, and re-layouts  16.3 us (15%)
  waiting for transfers between devices  12.4 us (11%)
  matrix products  3.59 us (3%)
  other arithmetic  1.96 us (2%)
  between operations  1.64 us (2%)
    pallas_call x1, Pallas kernels, cached_attention(): pl.pallas_call(cached_kernel, grid_spec=pltpu.PrefetchScalarGridSpec(num_...  32.8 us
    ppermute x3, starting transfers between devices, on_device(): received.append(lax.ppermute(sent[-1], 'rep', shift(outer - d)))  20.8 us
    unnamed x12, local copies, waits for them, and re-layouts  12.6 us
    pallas_call x1, Pallas kernels, final_attention(): pl.pallas_call(final_kernel, grid_spec=pltpu.PrefetchScalarGridSpec(num_s...  8.45 us
    ppermute x3, waiting for transfers between devices, on_device(): got = lax.ppermute(piece, 'rep', [(r, r ^ k) for r in range(replicas)])  7.8 us
    ppermute x3, starting transfers between devices, on_device(): lax.ppermute(columns(lax.rem(plane + d, outer)), 'rep', shift(d))  5.18 us
    ppermute x3, waiting for transfers between devices, on_device(): lax.ppermute(columns(lax.rem(plane + d, outer)), 'rep', shift(d))  4.54 us
    ppermute x3, starting transfers between devices, on_device(): got = lax.ppermute(piece, 'rep', [(r, r ^ k) for r in range(replicas)])  4.11 us
  transfers between devices with their start and end apart: 10, of which 2 were waited for; matrix products, arithmetic and copies ran while one was open for 18% of the time, Pallas kernels for 30%

profile of v2, /device:TPU:0, one launch (start us, length us, event | category | flops | bytes accessed | tf_op | source)
XLA Modules:
  0.0 107.8 jit_solution(11708270364599664813)
XLA Ops:
  0.6 1.5 %reshape.26 = bf16[128,2560]{1,0:T(8,128)(2,1)S(1)} reshape(bf16[32,4,2560]{2,1,0:T(4,128)(2,1)} %param.8) | data formatting | bytes 1310720 | tf_op jit(solution)/shard_map/reshape | solution.py:182
  2.1 0.5 collective-permute-start
  2.7 1.2 %copy.12 = bf16[40,8,2,512]{3,1,2,0:T(8,128)(2,1)S(1)} copy(bf16[40,8,2,512]{3,2,1,0:T(2,128)(2,1)} %bitcast.21) | data formatting | bytes 1310720
  3.8 2.6 %collective-permute-start.2 = (bf16[320,1024]{1,0:T(8,128)(2,1)S(1)}, bf16[320,1024]{1,0:T(8,128)(2,1)S(1)}, u32[]{:S(2)}, u32[]{:S(2)}) collective-permute-start(bf16[320,1024]{1,0:T(8,128)(2,1)S(1)} %bitcast.17), channel_id=1, source_target_pairs={{0,2},{2,0},{4,6},{6,4},{8,10},{10,8},{12,14},{14,12},{16,18},{18,... | collective-permute-start | bytes 1966088 | tf_op jit(solution)/shard_map/ppermute | solution.py:179
  6.4 1.5 %collective-permute-start.3 = (bf16[320,1024]{1,0:T(8,128)(2,1)S(1)}, bf16[320,1024]{1,0:T(8,128)(2,1)S(1)}, u32[]{:S(2)}, u32[]{:S(2)}) collective-permute-start(bf16[320,1024]{1,0:T(8,128)(2,1)S(1)} %bitcast.18), channel_id=1, source_target_pairs={{0,4},{2,6},{4,0},{6,2},{8,12},{10,14},{12,8},{14,10},{16,20},{18,... | collective-permute-start | bytes 1966088 | tf_op jit(solution)/shard_map/ppermute | solution.py:179
  7.9 11.4 %copy.13 = bf16[640,8,2,512]{3,1,2,0:T(8,128)(2,1)} copy(bf16[640,8,2,512]{3,2,1,0:T(2,128)(2,1)} %bitcast.16) | data formatting | bytes 20971520
  20.0 0.3 broadcast_in_dim.8
  20.4 0.1 constant_dynamic-update-slice_fusion.3
  20.4 0.1 broadcast_in_dim.7
  20.6 0.1 constant_dynamic-update-slice_fusion.5
  20.6 1.3 %constant_dynamic-update-slice_fusion.4 = bf16[128,5120]{1,0:T(8,128)(2,1)S(1)} fusion(bf16[128,5120]{1,0:T(8,128)(2,1)S(1)} %constant_dynamic-update-slice_fusion.5, bf16[128,2560]{1,0:T(8,128)(2,1)} %collective-permute-done, s32[]{:T(128)S(6)} %select_n.42), kind=kLoop, calls=%fused_computation.18 | loop fusion | bytes 1310724 | tf_op jit(solution)/shard_map/dynamic_update_slice | solution.py:188
  22.0 0.3 fusion
  22.3 0.3 fusion.1
  22.6 0.1 constant_dynamic-slice_fusion
  22.7 4.1 %collective-permute-start.6 = (bf16[128,1280]{1,0:T(8,128)(2,1)S(1)}, bf16[128,1280]{1,0:T(8,128)(2,1)S(1)}, u32[]{:S(2)}, u32[]{:S(2)}) collective-permute-start(bf16[128,1280]{1,0:T(8,128)(2,1)S(1)} %get-tuple-element.14), channel_id=1, source_target_pairs={{0,24},{2,26},{4,28},{6,30},{8,0},{10,2},{12,4},{14,6},{16,8},{18,... | collective-permute-start | bytes 983048 | tf_op jit(solution)/shard_map/ppermute | solution.py:206
  26.8 1.5 %fusion.5.sk.sv = f32[128,1024]{1,0:T(8,128)S(1)} fusion(bf16[128,5120]{1,0:T(8,128)(2,1)S(1)} %fusion.1, bf16[5120,1024]{1,0:T(8,128)(2,1)S(1)} %bitcast.15), kind=kOutput, calls=%fused_computation.21 | convolution fusion | flops 1342177280 | bytes 12320768 | tf_op jit(solution)/shard_map/dot_general | solution.py:216
  28.4 1.1 collective-permute-start.1
  29.5 7.8 %collective-permute-done.3 = bf16[320,1024]{1,0:T(8,128)(2,1)S(1)} collective-permute-done((bf16[320,1024]{1,0:T(8,128)(2,1)S(1)}, bf16[320,1024]{1,0:T(8,128)(2,1)S(1)}, u32[]{:S(2)}, u32[]{:S(2)}) %collective-permute-start.3) | collective-permute-done | bytes 655392 | tf_op jit(solution)/shard_map/ppermute | solution.py:179
  37.4 0.1 constant_dynamic-update-slice_fusion
  37.4 0.5 convolution_convert_fusion.rest_2_
  38.0 20.5 %collective-permute-start.9 = (bf16[128,1024]{1,0:T(8,128)(2,1)S(1)}, bf16[128,1024]{1,0:T(8,128)(2,1)S(1)}, u32[]{:S(2)}, u32[]{:S(2)}) collective-permute-start(bf16[128,1024]{1,0:T(8,128)(2,1)S(1)} %convolution_convert_fusion.rest_2_), channel_id=1, source_target_pairs={{0,8},{2,10},{4,12},{6,14},{8,16},{10,18},{12,20},{14,22},{16,24},... | collective-permute-start | bytes 786440 | tf_op jit(solution)/shard_map/ppermute | solution.py:213
  58.5 4.5 %collective-permute-done.5 = bf16[128,1280]{1,0:T(8,128)(2,1)S(1)} collective-permute-done((bf16[128,1280]{1,0:T(8,128)(2,1)S(1)}, bf16[128,1280]{1,0:T(8,128)(2,1)S(1)}, u32[]{:S(2)}, u32[]{:S(2)}) %collective-permute-start.5) | collective-permute-done | bytes 327712 | tf_op jit(solution)/shard_map/ppermute | solution.py:206
  63.0 0.5 convolution_convert_fusion.1.rest_1_
  63.6 0.1 collective-permute-start.8
  63.7 0.5 convolution_convert_fusion.2.rest_0_
  64.2 0.2 collective-permute-start.7
  64.4 0.5 fusion.2.ok.ov
  65.0 32.8 %shard_map.95 = (bf16[32,4,32,128]{3,2,1,0:T(8,128)(2,1)S(1)}, f32[32,4,32,128]{3,2,1,0:T(8,128)S(1)}, f32[32,4,32,128]{3,2,1,0:T(8,128)S(1)}) custom-call(s32[32]{0:T(128)S(1)} %copy-done.1, bf16[32,4,4096]{2,1,0:T(4,128)(2,1)S(1)} %copy-done, bf16[32,256,512]{2,1,0:T(8,128)(2,1)S(1)} %bitcast.14, bf16[32,256,512]{2,1,0:T(8,128)(2,1)} %v_ref.1, ...), custom_call_target="tpu_custom_call" | custom-call | flops 536870912 | bytes 24117248 | tf_op jit(solution)/shard_map/pallas_call | solution.py:59
  97.9 8.5 %shard_map.96 = (bf16[32,4,4096]{2,1,0:T(4,128)(2,1)}, bf16[128,512]{1,0:T(8,128)(2,1)S(1)}, bf16[128,512]{1,0:T(8,128)(2,1)S(1)}) custom-call(s32[1]{0:T(128)S(6)} %copy.20.adopt, bf16[32,4,32,128]{3,2,1,0:T(8,128)(2,1)S(1)} %get-tuple-element.8.qr_ref, f32[32,4,32,128]{3,2,1,0:T(8,128)S(1)} %get-tuple-element.9.acc_ref, ...), custom_call_target="tpu_custom_call" | custom-call | flops 268435456 | bytes 6291456 | tf_op jit(solution)/shard_map/pallas_call | solution.py:139
  106.3 0.1 stack.12
  106.4 0.1 stack.13
  106.5 1.3 %pad_maximum_fusion = bf16[32,4,2,512]{3,2,1,0:T(2,128)(2,1)} fusion(bf16[32,4,1,512]{3,2,1,0:T(2,128)(2,1)S(1)} %stack.13, bf16[32,4,1,512]{3,2,1,0:T(2,128)(2,1)S(1)} %stack.12), kind=kLoop, calls=%fused_computation.9 | loop fusion | flops 524288 | bytes 524288 | tf_op jit(solution)/shard_map/stack | solution.py:219
  (24 shorter events, 0.2 us)
Async XLA Ops:
  2.1 18.5 %collective-permute-start = (bf16[128,2560]{1,0:T(8,128)(2,1)S(1)}, bf16[128,2560]{1,0:T(8,128)(2,1)}, u32[]{:S(2)}, u32[]{:S(2)}) collective-permute-start(bf16[128,2560]{1,0:T(8,128)(2,1)S(1)} %reshape.26), channel_id=1, source_target_pairs={{0,1},{1,0},{2,3},{3,2},{4,5},{5,4},{6,7},{7,6},{8,9},{9,8},{10,11... | collective-permute-start | bytes 1966088 | tf_op jit(solution)/shard_map/ppermute | solution.py:187
  3.8 24.5 %collective-permute-start.2 = (bf16[320,1024]{1,0:T(8,128)(2,1)S(1)}, bf16[320,1024]{1,0:T(8,128)(2,1)S(1)}, u32[]{:S(2)}, u32[]{:S(2)}) collective-permute-start(bf16[320,1024]{1,0:T(8,128)(2,1)S(1)} %bitcast.17), channel_id=1, source_target_pairs={{0,2},{2,0},{4,6},{6,4},{8,10},{10,8},{12,14},{14,12},{16,18},{18,... | collective-permute-start | bytes 1966088 | tf_op jit(solution)/shard_map/ppermute | solution.py:179
  6.4 30.9 %collective-permute-start.3 = (bf16[320,1024]{1,0:T(8,128)(2,1)S(1)}, bf16[320,1024]{1,0:T(8,128)(2,1)S(1)}, u32[]{:S(2)}, u32[]{:S(2)}) collective-permute-start(bf16[320,1024]{1,0:T(8,128)(2,1)S(1)} %bitcast.18), channel_id=1, source_target_pairs={{0,4},{2,6},{4,0},{6,2},{8,12},{10,14},{12,8},{14,10},{16,20},{18,... | collective-permute-start | bytes 1966088 | tf_op jit(solution)/shard_map/ppermute | solution.py:179
  7.9 29.4 %collective-permute-start.4 = (bf16[320,1024]{1,0:T(8,128)(2,1)S(1)}, bf16[320,1024]{1,0:T(8,128)(2,1)S(1)}, u32[]{:S(2)}, u32[]{:S(2)}) collective-permute-start(bf16[320,1024]{1,0:T(8,128)(2,1)S(1)} %bitcast.19), channel_id=1, source_target_pairs={{0,6},{2,4},{4,2},{6,0},{8,14},{10,12},{12,10},{14,8},{16,22},{18,... | collective-permute-start | bytes 1966088 | tf_op jit(solution)/shard_map/ppermute | solution.py:179
  20.4 6.5 %copy-start.2 = (bf16[640,8,2,512]{3,1,2,0:T(8,128)(2,1)S(1)}, bf16[640,8,2,512]{3,1,2,0:T(8,128)(2,1)}, u32[]{:S(2)}) copy-start(bf16[640,8,2,512]{3,1,2,0:T(8,128)(2,1)} %copy.13) | copy-start | bytes 31457284
  22.7 14.7 %collective-permute-start.6 = (bf16[128,1280]{1,0:T(8,128)(2,1)S(1)}, bf16[128,1280]{1,0:T(8,128)(2,1)S(1)}, u32[]{:S(2)}, u32[]{:S(2)}) collective-permute-start(bf16[128,1280]{1,0:T(8,128)(2,1)S(1)} %get-tuple-element.14), channel_id=1, source_target_pairs={{0,24},{2,26},{4,28},{6,30},{8,0},{10,2},{12,4},{14,6},{16,8},{18,... | collective-permute-start | bytes 983048 | tf_op jit(solution)/shard_map/ppermute | solution.py:206
  26.8 36.2 %collective-permute-start.5 = (bf16[128,1280]{1,0:T(8,128)(2,1)S(1)}, bf16[128,1280]{1,0:T(8,128)(2,1)S(1)}, u32[]{:S(2)}, u32[]{:S(2)}) collective-permute-start(bf16[128,1280]{1,0:T(8,128)(2,1)S(1)} %get-tuple-element.15), channel_id=1, source_target_pairs={{0,16},{2,18},{4,20},{6,22},{8,24},{10,26},{12,28},{14,30},{16,0},... | collective-permute-start | bytes 983048 | tf_op jit(solution)/shard_map/ppermute | solution.py:206
  28.4 35.3 %collective-permute-start.1 = (bf16[128,1280]{1,0:T(8,128)(2,1)S(1)}, bf16[128,1280]{1,0:T(8,128)(2,1)S(1)}, u32[]{:S(2)}, u32[]{:S(2)}) collective-permute-start(bf16[128,1280]{1,0:T(8,128)(2,1)S(1)} %get-tuple-element.16), channel_id=1, source_target_pairs={{0,8},{2,10},{4,12},{6,14},{8,16},{10,18},{12,20},{14,22},{16,24},... | collective-permute-start | bytes 983048 | tf_op jit(solution)/shard_map/ppermute | solution.py:206
  37.3 27.7 %slice-start = ((s8[8388608]{0:T(1024)(128)(4,1)}), s8[4194304]{0:T(1024)(128)(4,1)S(1)}, s32[]{:S(2)}) async-start(s8[8388608]{0:T(1024)(128)(4,1)} %bitcast.13), calls=%async_computation | async-start | bytes 8388608
  38.0 27.0 %slice-start.1 = ((s8[8388608]{0:T(1024)(128)(4,1)}), s8[4194304]{0:T(1024)(128)(4,1)S(1)}, s32[]{:S(2)}) async-start(s8[8388608]{0:T(1024)(128)(4,1)} %bitcast.13), calls=%async_computation.1 | async-start | bytes 8388608
  38.0 59.9 %collective-permute-start.9 = (bf16[128,1024]{1,0:T(8,128)(2,1)S(1)}, bf16[128,1024]{1,0:T(8,128)(2,1)S(1)}, u32[]{:S(2)}, u32[]{:S(2)}) collective-permute-start(bf16[128,1024]{1,0:T(8,128)(2,1)S(1)} %convolution_convert_fusion.rest_2_), channel_id=1, source_target_pairs={{0,8},{2,10},{4,12},{6,14},{8,16},{10,18},{12,20},{14,22},{16,24},... | collective-permute-start | bytes 786440 | tf_op jit(solution)/shard_map/ppermute | solution.py:213
  63.6 1.4 %copy-start = (bf16[32,4,4096]{2,1,0:T(4,128)(2,1)S(1)}, bf16[32,4,4096]{2,1,0:T(4,128)(2,1)}, u32[]{:S(2)}) copy-start(bf16[32,4,4096]{2,1,0:T(4,128)(2,1)} %q_ref.1) | copy-start | bytes 3145732
  63.6 1.4 %copy-start.1 = (s32[32]{0:T(128)S(1)}, s32[32]{0:T(128)}, u32[]{:S(2)}) copy-start(s32[32]{0:T(128)} %lengths.1) | copy-start | bytes 388
  63.6 34.3 %collective-permute-start.8 = (bf16[128,1024]{1,0:T(8,128)(2,1)S(1)}, bf16[128,1024]{1,0:T(8,128)(2,1)S(1)}, u32[]{:S(2)}, u32[]{:S(2)}) collective-permute-start(bf16[128,1024]{1,0:T(8,128)(2,1)S(1)} %convolution_convert_fusion.1.rest_1_), channel_id=1, source_target_pairs={{0,16},{2,18},{4,20},{6,22},{8,24},{10,26},{12,28},{14,30},{16,0},... | collective-permute-start | bytes 786440 | tf_op jit(solution)/shard_map/ppermute | solution.py:213
  64.2 33.7 %collective-permute-start.7 = (bf16[128,1024]{1,0:T(8,128)(2,1)S(1)}, bf16[128,1024]{1,0:T(8,128)(2,1)S(1)}, u32[]{:S(2)}, u32[]{:S(2)}) collective-permute-start(bf16[128,1024]{1,0:T(8,128)(2,1)S(1)} %convolution_convert_fusion.2.rest_0_), channel_id=1, source_target_pairs={{0,24},{2,26},{4,28},{6,30},{8,0},{10,2},{12,4},{14,6},{16,8},{18,... | collective-permute-start | bytes 786440 | tf_op jit(solution)/shard_map/ppermute | solution.py:213

commit v3 on v2

--- a/solution.py
+++ b/solution.py
@@ -16,13 +16,13 @@
 epsilon = 1e-06
 
 
-def cached_kernel(lengths, q_ref, k_ref, v_ref, *rest):
+def cached_kernel(start, lengths, q_ref, k_ref, v_ref, *rest):
     qr_ref, acc_ref, stat_ref = rest[-3:]
     rows, steps = q_ref.shape[:2]
     context = k_ref.shape[1]
     heads = k_ref.shape[2] // HEAD
     per = q_ref.shape[2] // (heads * HEAD)
-    first = pl.program_id(0) * rows
+    first = start + pl.program_id(0) * rows
     position = lax.broadcasted_iota(jnp.int32, (per * steps, context), 1)
     lane = lax.broadcasted_iota(jnp.int32, (per * steps, HEAD), 1)
     for r in range(rows):
@@ -48,21 +48,22 @@
             stat_ref[r, h] = jnp.where(lane < HEAD // 2, highest, total)
 
 
-def cached_attention(queries, key_cache, value_cache, lengths, after):
+def cached_attention(queries, key_cache, value_cache, lengths, start, taken, after, held):
     rows, steps, width = queries.shape
     context, local = key_cache.shape[1:]
     heads = local // HEAD
     count = width // (heads * HEAD) * steps
-    some = 4 if rows % 4 == 0 else 1
-    block = lambda *shape: pl.BlockSpec((some,) + shape, lambda r, n: (r,) + (0,) * len(shape))
+    some = 4 if start % 4 == 0 and taken % 4 == 0 else 1
+    skip = start // some
+    block = lambda *shape: pl.BlockSpec((some,) + shape, lambda r, n: (skip + r,) + (0,) * len(shape))
     piece = (rows, heads, count, HEAD)
     return pl.pallas_call(
-        cached_kernel,
+        functools.partial(cached_kernel, start),
         grid_spec=pltpu.PrefetchScalarGridSpec(
             num_scalar_prefetch=1,
-            grid=(rows // some,),
+            grid=(taken // some,),
             in_specs=[block(steps, width), block(context, local), block(context, local)]
-            + [pl.BlockSpec(memory_space=pl.ANY)] * len(after),
+            + [pl.BlockSpec(memory_space=pl.ANY)] * (len(after) + len(held)),
             out_specs=[block(heads, count, HEAD)] * 3,
         ),
         out_shape=(
@@ -70,16 +71,17 @@
             jax.ShapeDtypeStruct(piece, jnp.float32),
             jax.ShapeDtypeStruct(piece, jnp.float32),
         ),
+        input_output_aliases={4 + len(after) + i: i for i in range(len(held))},
         compiler_params=pltpu.CompilerParams(vmem_limit_bytes=32 * 1024 * 1024),
         cost_estimate=pl.CostEstimate(
-            flops=4 * rows * heads * count * context * HEAD,
-            bytes_accessed=4 * rows * context * local + 14 * rows * heads * count * HEAD,
-            transcendentals=rows * heads * count * context,
-        ),
-    )(lengths, queries, key_cache, value_cache, *after)
-
-
-def final_kernel(adopt, qr_ref, acc_ref, stat_ref, sk, sv, ok, ov, *rest):
+            flops=4 * taken * heads * count * context * HEAD,
+            bytes_accessed=4 * taken * context * local + 14 * taken * heads * count * HEAD,
+            transcendentals=taken * heads * count * context,
+        ),
+    )(lengths, queries, key_cache, value_cache, *after, *held)
+
+
+def final_kernel(adopt, qr_ref, acc_ref, stat_ref, norm_ref, sk, sv, ok, ov, *rest):
     out_ref, nk_ref, nv_ref = rest[-3:]
     received = rest[:-3]
     rows, _, count, _ = qr_ref.shape
@@ -92,8 +94,8 @@
     for d in range(len(received) // 2):
         current_k = current_k + received[2 * d][...].astype(jnp.float32)
         current_v = current_v + received[2 * d + 1][...].astype(jnp.float32)
-    keys = jnp.where(fresh, current_k, sk[...])
-    values = jnp.where(fresh, current_v, sv[...])
+    keys = jnp.where(fresh, current_k * norm_ref[...], sk[...])
+    values = jnp.where(fresh, current_v * norm_ref[...], sv[...])
     keys = keys * lax.rsqrt(jnp.mean(keys * keys, axis=-1, keepdims=True) + epsilon)
     keys = keys.astype(jnp.bfloat16)
     values = values.astype(jnp.bfloat16)
@@ -127,7 +129,7 @@
         )
 
 
-def final_attention(adopt, qr, acc, stat, stale, own, received):
+def final_attention(adopt, qr, acc, stat, norm, stale, own, received):
     rows, heads, count, _ = qr.shape
     flat, both = stale.shape
     steps = flat // rows
@@ -141,7 +143,7 @@
         grid_spec=pltpu.PrefetchScalarGridSpec(
             num_scalar_prefetch=1,
             grid=(heads,),
-            in_specs=[piece] * 3 + [key, value] * (2 + len(received)),
+            in_specs=[piece] * 3 + [pl.BlockSpec((flat, HEAD), lambda h, n: (0, 0))] + [key, value] * (2 + len(received)),
             out_specs=[
                 pl.BlockSpec((rows, steps, per * HEAD), lambda h, n: (0, 0, h)),
                 key,
@@ -159,7 +161,7 @@
             bytes_accessed=12 * rows * heads * count * HEAD,
             transcendentals=rows * heads * count * flat,
         ),
-    )(adopt, qr, acc, stat, stale, stale, own, own, *doubled)
+    )(adopt, qr, acc, stat, norm, stale, stale, own, own, *doubled)
 
 
 def on_device(replicas, parts, hidden, queries, key_cache, value_cache, lengths, adopt, old_kv, fresh_kv):
@@ -181,29 +183,44 @@
 
     mine = hidden.reshape(flat, share)
     me = lax.axis_index("tp")
+    depth = width // outer
+    planes = outer // parts
+
+    def shift(d):
+        return [
+            (z * GROUP + p, (z + d) % outer * GROUP + p) for z in range(outer) for p in range(GROUP)
+        ]
+
+    def holders(d):
+        pairs = []
+        for source, target in shift(d):
+            t = target // GROUP // planes
+            pairs.append((source * parts + t, target * parts + t))
+        return pairs
+
+    inputs = []
+    for d in range(outer):
+        z = lax.rem(plane + d, outer)
+        block = lax.dynamic_slice(mine, (0, lax.rem(z, planes) * depth), (flat, depth))
+        if d == 0:
+            block = jnp.where(me == plane // planes, block, jnp.zeros_like(block))
+        else:
+            block = lax.ppermute(block, ("rep", "tp"), holders(d))
+        inputs.append(block)
+    if parts == 2:
+        inputs = [block + lax.ppermute(block, "tp", [(0, 1), (1, 0)]) for block in inputs]
+    else:
+        inputs = [lax.psum(block, "tp") for block in inputs]
+
     whole = jnp.zeros((flat, width), jnp.bfloat16)
     whole = lax.dynamic_update_slice(whole, mine, (0, me * share))
     for d in range(1, parts):
         got = lax.ppermute(mine, "tp", [(t, (t + d) % parts) for t in range(parts)])
         whole = lax.dynamic_update_slice(whole, got, (0, lax.rem(me - d + parts, parts) * share))
     widened = whole.astype(jnp.float32)
-    normed = (
-        widened * lax.rsqrt(jnp.mean(widened * widened, axis=-1, keepdims=True) + epsilon)
-    ).astype(jnp.bfloat16)
-
-    depth = width // outer
-
-    def shift(d):
-        return [
-            (z * GROUP + p, (z + d) % outer * GROUP + p) for z in range(outer) for p in range(GROUP)
-        ]
-
-    def columns(z):
-        return lax.dynamic_slice(normed, (0, z * depth), (flat, depth))
-
-    inputs = [columns(plane)]
-    for d in range(1, outer):
-        inputs.append(lax.ppermute(columns(lax.rem(plane + d, outer)), "rep", shift(d)))
+    norm = lax.rsqrt(jnp.mean(widened * widened, axis=-1, keepdims=True) + epsilon)
+    normed = (widened * norm).astype(jnp.bfloat16)
+
     own = jnp.dot(inputs[0], weights, preferred_element_type=jnp.float32)
     received = []
     sent = []
@@ -212,10 +229,14 @@
         sent.append(partial.astype(jnp.bfloat16))
         received.append(lax.ppermute(sent[-1], "rep", shift(outer - d)))
 
-    old_kv, _ = lax.optimization_barrier((old_kv, normed[:1, :1]))
     stale = jnp.dot(normed, old_kv.reshape(width, both), preferred_element_type=jnp.float32)
-    qr, acc, stat = cached_attention(queries, key_cache, value_cache, lengths, sent)
-    attended, keys, values = final_attention(adopt, qr, acc, stat, stale, own, received)
+    early = 3 * rows // 8
+    held = cached_attention(queries, key_cache, value_cache, lengths, 0, early, [], ())
+    qr, acc, stat = cached_attention(
+        queries, key_cache, value_cache, lengths, early, rows - early, sent, held
+    )
+    norm = jnp.broadcast_to(norm, (flat, HEAD))
+    attended, keys, values = final_attention(adopt, qr, acc, stat, norm, stale, own, received)
     appended = jnp.stack([keys, values], axis=1).reshape(rows, steps, 2, both // 2)
     return attended, appended
 

time: 108 us -> 114 us (1.056)
  local copies, waits for them, and re-layouts: 16.3 us -> 28.7 us
  starting transfers between devices: 30.6 us -> 19.8 us
  matrix products: 3.59 us -> 11 us
  waiting for transfers between devices: 12.4 us -> 6.22 us
  Pallas kernels: 41.3 us -> 43.4 us
    ppermute x3, starting transfers between devices: 20.8 us -> 4.17 us  [on_device(): received.append(lax.ppermute(sent[-1], 'rep', shift(outer - d)))]
    ppermute x3, waiting for transfers between devices: 7.8 us -> 0.01 us  [on_device(): got = lax.ppermute(piece, 'rep', [(r, r ^ k) for r in range(replicas)])]
    dynamic_update_slice x3, local copies, waits for them, and re-layouts: 0.15 us -> 5.97 us  [on_device(): weights = lax.dynamic_update_slice(weights, got, ((spot ^ k) * count, 0))]
    dot_general x3, matrix products: 1.55 us -> 7.15 us  [on_device(): partial = jnp.dot(inputs[d], weights, preferred_element_type=jnp.float32)]
    ppermute x3 -> x7, starting transfers between devices: 5.18 us -> 10.6 us  [the longest x3 9.99 us: on_device(): block = lax.ppermute(block, ('rep', 'tp'), holders(d))]
    unnamed x12 -> x18, local copies, waits for them, and re-layouts: 12.6 us -> 16.9 us
    pallas_call x1 -> x2, Pallas kernels: 32.8 us -> 34.9 us  [cached_attention(): pl.pallas_call(functools.partial(cached_kernel, start), grid_spec=pltpu.P...]
    dynamic_update_slice x1, local copies, waits for them, and re-layouts: 0.05 us -> 1.99 us  [on_device(): weights = lax.dynamic_update_slice(weights, piece, (spot * count, 0))]
  transfers between devices with their start and end apart: 10 -> 14, of which waited for: 2 -> 1; matrix products, arithmetic and copies ran while one was open for 18% -> 31% of each run, Pallas kernels for 30% -> 31%
where the time goes in v3:
time: 114 us; the launch traced here: 113 us
  Pallas kernels  43.4 us (38%)
  local copies, waits for them, and re-layouts  28.7 us (25%)
  starting transfers between devices  19.8 us (17%)
  matrix products  11 us (10%)
  waiting for transfers between devices  6.22 us (5%)
  other arithmetic  2.61 us (2%)
  between operations  1.61 us (1%)
    pallas_call x2, Pallas kernels, cached_attention(): pl.pallas_call(functools.partial(cached_kernel, start), grid_spec=pltpu.P...  34.9 us
    unnamed x18, local copies, waits for them, and re-layouts  16.9 us
    ppermute x3, starting transfers between devices, on_device(): block = lax.ppermute(block, ('rep', 'tp'), holders(d))  9.99 us
    pallas_call x1, Pallas kernels, final_attention(): pl.pallas_call(final_kernel, grid_spec=pltpu.PrefetchScalarGridSpec(num_s...  8.48 us
    dot_general x3, matrix products, on_device(): partial = jnp.dot(inputs[d], weights, preferred_element_type=jnp.float32)  7.15 us
    ppermute x3, waiting for transfers between devices, on_device(): block = lax.ppermute(block, ('rep', 'tp'), holders(d))  6.19 us
    dynamic_update_slice x3, local copies, waits for them, and re-layouts, on_device(): weights = lax.dynamic_update_slice(weights, got, ((spot ^ k) * count, 0))  5.97 us
    ppermute x3, starting transfers between devices, on_device(): got = lax.ppermute(piece, 'rep', [(r, r ^ k) for r in range(replicas)])  4.46 us
  transfers between devices with their start and end apart: 14, of which 1 were waited for; matrix products, arithmetic and copies ran while one was open for 31% of the time, Pallas kernels for 31%

profile of v3, /device:TPU:0, one launch (start us, length us, event | category | flops | bytes accessed | tf_op | source)
XLA Modules:
  0.0 113.2 jit_solution(7273097544609454270)
XLA Ops:
  0.6 2.0 %copy.15 = bf16[40,8,2,512]{3,1,2,0:T(8,128)(2,1)} copy(bf16[40,8,2,512]{3,2,1,0:T(2,128)(2,1)} %bitcast.13) | data formatting | bytes 1310720
  2.7 2.9 %collective-permute-start.2 = (bf16[320,1024]{1,0:T(8,128)(2,1)}, bf16[320,1024]{1,0:T(8,128)(2,1)}, u32[]{:S(2)}, u32[]{:S(2)}) collective-permute-start(bf16[320,1024]{1,0:T(8,128)(2,1)} %bitcast.1), channel_id=1, source_target_pairs={{0,2},{2,0},{4,6},{6,4},{8,10},{10,8},{12,14},{14,12},{16,18},{18,... | collective-permute-start | bytes 1966088 | tf_op jit(solution)/shard_map/ppermute | solution.py:181
  5.6 1.5 %collective-permute-start.3 = (bf16[320,1024]{1,0:T(8,128)(2,1)}, bf16[320,1024]{1,0:T(8,128)(2,1)}, u32[]{:S(2)}, u32[]{:S(2)}) collective-permute-start(bf16[320,1024]{1,0:T(8,128)(2,1)} %bitcast.1), channel_id=1, source_target_pairs={{0,4},{2,6},{4,0},{6,2},{8,12},{10,14},{12,8},{14,10},{16,20},{18,... | collective-permute-start | bytes 1966088 | tf_op jit(solution)/shard_map/ppermute | solution.py:181
  7.1 1.5 %reshape.26 = bf16[128,2560]{1,0:T(8,128)(2,1)S(1)} reshape(bf16[32,4,2560]{2,1,0:T(4,128)(2,1)} %param.8) | data formatting | bytes 1310720 | tf_op jit(solution)/shard_map/reshape | solution.py:184
  8.6 1.0 dynamic-slice_select_fusion
  9.6 1.3 %collective-permute-start.7 = (bf16[128,1280]{1,0:T(8,128)(2,1)S(1)}, bf16[128,1280]{1,0:T(8,128)(2,1)S(1)}, u32[]{:S(2)}, u32[]{:S(2)}) collective-permute-start(bf16[128,1280]{1,0:T(8,128)(2,1)S(1)} %get-tuple-element.21), channel_id=1, source_target_pairs={{1,25},{3,27},{5,29},{7,31},{8,0},{10,2},{12,4},{14,6},{16,8},{18,... | collective-permute-start | bytes 983048 | tf_op jit(solution)/shard_map/ppermute | solution.py:208
  10.9 1.3 %collective-permute-start.5 = (bf16[128,1280]{1,0:T(8,128)(2,1)}, bf16[128,1280]{1,0:T(8,128)(2,1)}, u32[]{:S(2)}, u32[]{:S(2)}) collective-permute-start(bf16[128,1280]{1,0:T(8,128)(2,1)} %get-tuple-element.22), channel_id=1, source_target_pairs={{1,17},{3,19},{5,21},{7,23},{9,25},{11,27},{13,29},{15,31},{16,0},... | collective-permute-start | bytes 983048 | tf_op jit(solution)/shard_map/ppermute | solution.py:208
  12.2 0.1 broadcast_in_dim.16
  12.4 6.2 %collective-permute-done.7 = bf16[128,1280]{1,0:T(8,128)(2,1)S(1)} collective-permute-done((bf16[128,1280]{1,0:T(8,128)(2,1)S(1)}, bf16[128,1280]{1,0:T(8,128)(2,1)S(1)}, u32[]{:S(2)}, u32[]{:S(2)}) %collective-permute-start.7) | collective-permute-done | bytes 327712 | tf_op jit(solution)/shard_map/ppermute | solution.py:208
  18.6 7.4 %collective-permute-start = (bf16[128,1280]{1,0:T(8,128)(2,1)}, bf16[128,1280]{1,0:T(8,128)(2,1)}, u32[]{:S(2)}, u32[]{:S(2)}) collective-permute-start(bf16[128,1280]{1,0:T(8,128)(2,1)} %get-tuple-element.23), channel_id=1, source_target_pairs={{0,8},{2,10},{4,12},{6,14},{9,17},{11,19},{13,21},{15,23},{17,25},... | collective-permute-start | bytes 983048 | tf_op jit(solution)/shard_map/ppermute | solution.py:208
  26.0 1.9 %broadcast_in_dim.15 = bf16[1280,1024]{1,0:T(8,128)(2,1)} broadcast(bf16[]{:T(256)} %constant.78.clone.1), dimensions={} | broadcast | bytes 2621442 | tf_op jit(solution)/shard_map/broadcast_in_dim | solution.py:178
  27.9 2.0 %constant_dynamic-update-slice_fusion.5 = bf16[1280,1024]{1,0:T(8,128)(2,1)} fusion(bf16[1280,1024]{1,0:T(8,128)(2,1)} %broadcast_in_dim.15, bf16[320,1024]{1,0:T(8,128)(2,1)} %bitcast.1, s32[]{:T(128)S(6)} %select_n.55), kind=kLoop, calls=%fused_computation.23 | loop fusion | bytes 1310724 | tf_op jit(solution)/shard_map/dynamic_update_slice | solution.py:179
  29.9 11.5 %copy.16 = bf16[640,8,2,512]{3,1,2,0:T(8,128)(2,1)} copy(bf16[640,8,2,512]{3,2,1,0:T(2,128)(2,1)} %bitcast.12) | data formatting | bytes 20971520
  42.1 3.4 %copy-done = bf16[32,256,512]{2,1,0:T(8,128)(2,1)S(1)} copy-done((bf16[32,256,512]{2,1,0:T(8,128)(2,1)S(1)}, bf16[32,256,512]{2,1,0:T(8,128)(2,1)}, u32[]{:S(2)}) %copy-start) | copy-done | bytes 8388632
  45.5 13.7 %shard_map.95 = (bf16[32,4,32,128]{3,2,1,0:T(8,128)(2,1)S(1)}, f32[32,4,32,128]{3,2,1,0:T(8,128)S(1)}, f32[32,4,32,128]{3,2,1,0:T(8,128)S(1)}) custom-call(s32[32]{0:T(128)S(1)} %copy-done.2, bf16[32,4,4096]{2,1,0:T(4,128)(2,1)S(1)} %copy-done.1, bf16[32,256,512]{2,1,0:T(8,128)(2,1)S(1)} %copy-done, bf16[32,256,512]{2,1,0:T(8,128)(2,1)} %v_ref.3), custom_call_target="tpu_custom_call" | custom-call | flops 201326592 | bytes 9043968 | tf_op jit(solution)/shard_map/pallas_call | solution.py:60
  59.2 0.1 collective-permute-start.8
  59.3 2.0 %constant_dynamic-update-slice_fusion.4 = bf16[1280,1024]{1,0:T(8,128)(2,1)} fusion(bf16[1280,1024]{1,0:T(8,128)(2,1)} %constant_dynamic-update-slice_fusion.5, bf16[320,1024]{1,0:T(8,128)(2,1)} %collective-permute-done.2, s32[]{:T(128)S(6)} %select_n.56), kind=kLoop, calls=%fused_computation.22 | loop fusion | bytes 1310724 | tf_op jit(solution)/shard_map/dynamic_update_slice | solution.py:182
  61.2 0.5 collective-permute-start.9
  61.7 2.0 %constant_dynamic-update-slice_fusion.3 = bf16[1280,1024]{1,0:T(8,128)(2,1)} fusion(bf16[1280,1024]{1,0:T(8,128)(2,1)} %constant_dynamic-update-slice_fusion.4, bf16[320,1024]{1,0:T(8,128)(2,1)} %collective-permute-done.3, s32[]{:T(128)S(6)} %select_n.57), kind=kLoop, calls=%fused_computation.21 | loop fusion | bytes 1310724 | tf_op jit(solution)/shard_map/dynamic_update_slice | solution.py:182
  63.7 0.5 collective-permute-start.6
  64.3 2.0 %constant_dynamic-update-slice_fusion.2 = bf16[1280,1024]{1,0:T(8,128)(2,1)} fusion(bf16[1280,1024]{1,0:T(8,128)(2,1)} %constant_dynamic-update-slice_fusion.3, bf16[320,1024]{1,0:T(8,128)(2,1)} %collective-permute-done.4, s32[]{:T(128)S(6)} %select_n.58), kind=kLoop, calls=%fused_computation.20 | loop fusion | bytes 1310724 | tf_op jit(solution)/shard_map/dynamic_update_slice | solution.py:182
  66.3 2.4 %convolution_convert_fusion.rest_2_ = bf16[128,1024]{1,0:T(8,128)(2,1)S(1)} fusion(bf16[1280,1024]{1,0:T(8,128)(2,1)} %constant_dynamic-update-slice_fusion.2, bf16[128,1280]{1,0:T(8,128)(2,1)S(1)} %copy-done.4, bf16[128,1280]{1,0:T(8,128)(2,1)S(1)} %collective-permute-done.8), kind=kOutput, calls=%fused_computation.6 | convolution fusion | flops 335839232 | bytes 3538944 | tf_op jit(solution)/shard_map/dot_general | solution.py:228
  68.8 2.4 %convolution_convert_fusion.1.rest_1_ = bf16[128,1024]{1,0:T(8,128)(2,1)S(1)} fusion(bf16[1280,1024]{1,0:T(8,128)(2,1)} %constant_dynamic-update-slice_fusion.2, bf16[128,1280]{1,0:T(8,128)(2,1)} %collective-permute-done.5, bf16[128,1280]{1,0:T(8,128)(2,1)S(1)} %collective-permute-done.6), kind=kOutput, calls=%fused_computation.7 | convolution fusion | flops 335839232 | bytes 3538944 | tf_op jit(solution)/shard_map/dot_general | solution.py:228
  71.3 0.3 fusion
  71.7 2.4 %convolution_convert_fusion.2.rest_0_ = bf16[128,1024]{1,0:T(8,128)(2,1)S(1)} fusion(bf16[1280,1024]{1,0:T(8,128)(2,1)} %constant_dynamic-update-slice_fusion.2, bf16[128,1280]{1,0:T(8,128)(2,1)} %collective-permute-done, bf16[128,1280]{1,0:T(8,128)(2,1)S(1)} %collective-permute-done.1), kind=kOutput, calls=%fused_computation.8 | convolution fusion | flops 335839232 | bytes 3538944 | tf_op jit(solution)/shard_map/dot_general | solution.py:228
  74.1 4.0 %collective-permute-start.11 = (bf16[128,1024]{1,0:T(8,128)(2,1)S(1)}, bf16[128,1024]{1,0:T(8,128)(2,1)S(1)}, u32[]{:S(2)}, u32[]{:S(2)}) collective-permute-start(bf16[128,1024]{1,0:T(8,128)(2,1)S(1)} %convolution_convert_fusion.2.rest_0_), channel_id=1, source_target_pairs={{0,24},{2,26},{4,28},{6,30},{8,0},{10,2},{12,4},{14,6},{16,8},{18,... | collective-permute-start | bytes 786440 | tf_op jit(solution)/shard_map/ppermute | solution.py:230
  78.1 1.6 %fusion.2.sk.sv = f32[128,1024]{1,0:T(8,128)S(1)} fusion(bf16[5120,1024]{1,0:T(8,128)(2,1)S(1)} %bitcast.11, bf16[128,5120]{1,0:T(8,128)(2,1)S(1)} %constant_dynamic-update-slice_fusion, f32[128]{0:T(128)S(1)} %add_rsqrt_fusion), kind=kOutput, calls=%fused_computation.4 | convolution fusion | flops 1344143360 | bytes 12321280 | tf_op jit(solution)/shard_map/dot_general | solution.py:232
  79.7 21.2 %shard_map.96 = (bf16[32,4,32,128]{3,2,1,0:T(8,128)(2,1)S(1)}, f32[32,4,32,128]{3,2,1,0:T(8,128)S(1)}, f32[32,4,32,128]{3,2,1,0:T(8,128)S(1)}) custom-call(s32[32]{0:T(128)S(1)} %copy-done.2, bf16[32,4,4096]{2,1,0:T(4,128)(2,1)S(1)} %copy-done.1, bf16[32,256,512]{2,1,0:T(8,128)(2,1)S(1)} %copy-done, ...), custom_call_target="tpu_custom_call", output_to_operand_aliasing={{0}: (7, {}), {1}: (8, {}), {2}: (9, {})} | custom-call | flops 335544320 | bytes 15073280 | tf_op jit(solution)/shard_map/pallas_call | solution.py:60
  100.9 2.3 %fusion.5.ok.ov = f32[128,1024]{1,0:T(8,128)S(1)} fusion(bf16[1280,1024]{1,0:T(8,128)(2,1)} %constant_dynamic-update-slice_fusion.2, bf16[128,1280]{1,0:T(8,128)(2,1)S(1)} %get-tuple-element.20, bf16[128,1280]{1,0:T(8,128)(2,1)S(1)} %collective-permute-done.10), kind=kOutput, calls=%fused_computation.9 | convolution fusion | flops 335708160 | bytes 3801088 | tf_op jit(solution)/shard_map/dot_general | solution.py:224
  103.2 0.1 broadcast_in_dim.17.norm_ref
  103.3 8.5 %shard_map.97 = (bf16[32,4,4096]{2,1,0:T(4,128)(2,1)}, bf16[128,512]{1,0:T(8,128)(2,1)S(1)}, bf16[128,512]{1,0:T(8,128)(2,1)S(1)}) custom-call(s32[1]{0:T(128)S(6)} %copy.26.adopt, bf16[32,4,32,128]{3,2,1,0:T(8,128)(2,1)S(1)} %get-tuple-element.14.qr_ref, f32[32,4,32,128]{3,2,1,0:T(8,128)S(1)} %get-tuple-element.15.acc_ref, ...), custom_call_target="tpu_custom_call" | custom-call | flops 268435456 | bytes 6291456 | tf_op jit(solution)/shard_map/pallas_call | solution.py:141
  111.9 1.3 %pad_maximum_fusion = bf16[32,4,2,512]{3,2,1,0:T(2,128)(2,1)} fusion(bf16[32,4,1,512]{3,2,1,0:T(2,128)(2,1)S(1)} %stack.13, bf16[32,4,1,512]{3,2,1,0:T(2,128)(2,1)S(1)} %stack.12), kind=kLoop, calls=%fused_computation.15 | loop fusion | flops 524288 | bytes 524288 | tf_op jit(solution)/shard_map/stack | solution.py:240
  (39 shorter events, 0.6 us)
Async XLA Ops:
  2.7 56.5 %collective-permute-start.2 = (bf16[320,1024]{1,0:T(8,128)(2,1)}, bf16[320,1024]{1,0:T(8,128)(2,1)}, u32[]{:S(2)}, u32[]{:S(2)}) collective-permute-start(bf16[320,1024]{1,0:T(8,128)(2,1)} %bitcast.1), channel_id=1, source_target_pairs={{0,2},{2,0},{4,6},{6,4},{8,10},{10,8},{12,14},{14,12},{16,18},{18,... | collective-permute-start | bytes 1966088 | tf_op jit(solution)/shard_map/ppermute | solution.py:181
  5.6 55.6 %collective-permute-start.3 = (bf16[320,1024]{1,0:T(8,128)(2,1)}, bf16[320,1024]{1,0:T(8,128)(2,1)}, u32[]{:S(2)}, u32[]{:S(2)}) collective-permute-start(bf16[320,1024]{1,0:T(8,128)(2,1)} %bitcast.1), channel_id=1, source_target_pairs={{0,4},{2,6},{4,0},{6,2},{8,12},{10,14},{12,8},{14,10},{16,20},{18,... | collective-permute-start | bytes 1966088 | tf_op jit(solution)/shard_map/ppermute | solution.py:181
  7.1 57.1 %collective-permute-start.4 = (bf16[320,1024]{1,0:T(8,128)(2,1)}, bf16[320,1024]{1,0:T(8,128)(2,1)}, u32[]{:S(2)}, u32[]{:S(2)}) collective-permute-start(bf16[320,1024]{1,0:T(8,128)(2,1)} %bitcast.1), channel_id=1, source_target_pairs={{0,6},{2,4},{4,2},{6,0},{8,14},{10,12},{12,10},{14,8},{16,22},{18,... | collective-permute-start | bytes 1966088 | tf_op jit(solution)/shard_map/ppermute | solution.py:181
  9.6 9.0 %collective-permute-start.7 = (bf16[128,1280]{1,0:T(8,128)(2,1)S(1)}, bf16[128,1280]{1,0:T(8,128)(2,1)S(1)}, u32[]{:S(2)}, u32[]{:S(2)}) collective-permute-start(bf16[128,1280]{1,0:T(8,128)(2,1)S(1)} %get-tuple-element.21), channel_id=1, source_target_pairs={{1,25},{3,27},{5,29},{7,31},{8,0},{10,2},{12,4},{14,6},{16,8},{18,... | collective-permute-start | bytes 983048 | tf_op jit(solution)/shard_map/ppermute | solution.py:208
  10.9 52.8 %collective-permute-start.5 = (bf16[128,1280]{1,0:T(8,128)(2,1)}, bf16[128,1280]{1,0:T(8,128)(2,1)}, u32[]{:S(2)}, u32[]{:S(2)}) collective-permute-start(bf16[128,1280]{1,0:T(8,128)(2,1)} %get-tuple-element.22), channel_id=1, source_target_pairs={{1,17},{3,19},{5,21},{7,23},{9,25},{11,27},{13,29},{15,31},{16,0},... | collective-permute-start | bytes 983048 | tf_op jit(solution)/shard_map/ppermute | solution.py:208
  18.6 11.3 %copy-start.3 = (bf16[128,1280]{1,0:T(8,128)(2,1)}, bf16[128,1280]{1,0:T(8,128)(2,1)S(1)}, u32[]{:S(2)}) copy-start(bf16[128,1280]{1,0:T(8,128)(2,1)S(1)} %collective-permute-done.7) | copy-start | bytes 983044
  18.6 45.1 %collective-permute-start = (bf16[128,1280]{1,0:T(8,128)(2,1)}, bf16[128,1280]{1,0:T(8,128)(2,1)}, u32[]{:S(2)}, u32[]{:S(2)}) collective-permute-start(bf16[128,1280]{1,0:T(8,128)(2,1)} %get-tuple-element.23), channel_id=1, source_target_pairs={{0,8},{2,10},{4,12},{6,14},{9,17},{11,19},{13,21},{15,23},{17,25},... | collective-permute-start | bytes 983048 | tf_op jit(solution)/shard_map/ppermute | solution.py:208
  29.9 12.1 %copy-start.1 = (bf16[32,4,4096]{2,1,0:T(4,128)(2,1)S(1)}, bf16[32,4,4096]{2,1,0:T(4,128)(2,1)}, u32[]{:S(2)}) copy-start(bf16[32,4,4096]{2,1,0:T(4,128)(2,1)} %q_ref.3) | copy-start | bytes 3145732
  29.9 12.1 %copy-start.2 = (s32[32]{0:T(128)S(1)}, s32[32]{0:T(128)}, u32[]{:S(2)}) copy-start(s32[32]{0:T(128)} %lengths.3) | copy-start | bytes 388
  42.1 3.4 %copy-start = (bf16[32,256,512]{2,1,0:T(8,128)(2,1)S(1)}, bf16[32,256,512]{2,1,0:T(8,128)(2,1)}, u32[]{:S(2)}) copy-start(bf16[32,256,512]{2,1,0:T(8,128)(2,1)} %k_ref.3) | copy-start | bytes 25165828
  45.5 13.7 %copy-start.4 = (bf16[128,1280]{1,0:T(8,128)(2,1)S(1)}, bf16[128,1280]{1,0:T(8,128)(2,1)}, u32[]{:S(2)}) copy-start(bf16[128,1280]{1,0:T(8,128)(2,1)} %copy-done.3) | copy-start | bytes 983044
  45.5 32.7 %slice-start = ((s8[10485760]{0:T(1024)(128)(4,1)}), s8[4194304]{0:T(1024)(128)(4,1)S(1)}, s32[]{:S(2)}) async-start(s8[10485760]{0:T(1024)(128)(4,1)} %bitcast.9), calls=%async_computation | async-start | bytes 8388608
  45.5 32.7 %slice-start.1 = ((s8[10485760]{0:T(1024)(128)(4,1)}), s8[4194304]{0:T(1024)(128)(4,1)S(1)}, s32[]{:S(2)}) async-start(s8[10485760]{0:T(1024)(128)(4,1)} %bitcast.9), calls=%async_computation.1 | async-start | bytes 8388608
  59.2 7.1 %collective-permute-start.8 = (bf16[128,1280]{1,0:T(8,128)(2,1)S(1)}, bf16[128,1280]{1,0:T(8,128)(2,1)S(1)}, u32[]{:S(2)}, u32[]{:S(2)}) collective-permute-start(bf16[128,1280]{1,0:T(8,128)(2,1)S(1)} %copy-done.4), channel_id=1, source_target_pairs={{0,1},{1,0},{2,3},{3,2},{4,5},{5,4},{6,7},{7,6},{8,9},{9,8},{10,11... | collective-permute-start | bytes 983048 | tf_op jit(solution)/shard_map/ppermute | solution.py:211
  61.2 10.0 %collective-permute-start.9 = (bf16[128,2560]{1,0:T(8,128)(2,1)S(1)}, bf16[128,2560]{1,0:T(8,128)(2,1)S(1)}, u32[]{:S(2)}, u32[]{:S(2)}) collective-permute-start(bf16[128,2560]{1,0:T(8,128)(2,1)S(1)} %reshape.26), channel_id=1, source_target_pairs={{0,1},{1,0},{2,3},{3,2},{4,5},{5,4},{6,7},{7,6},{8,9},{9,8},{10,11... | collective-permute-start | bytes 1966088 | tf_op jit(solution)/shard_map/ppermute | solution.py:218
  63.7 37.2 %collective-permute-start.10 = (bf16[128,1280]{1,0:T(8,128)(2,1)S(1)}, bf16[128,1280]{1,0:T(8,128)(2,1)S(1)}, u32[]{:S(2)}, u32[]{:S(2)}) collective-permute-start(bf16[128,1280]{1,0:T(8,128)(2,1)S(1)} %get-tuple-element.20), channel_id=1, source_target_pairs={{0,1},{1,0},{2,3},{3,2},{4,5},{5,4},{6,7},{7,6},{8,9},{9,8},{10,11... | collective-permute-start | bytes 983048 | tf_op jit(solution)/shard_map/ppermute | solution.py:211
  63.7 5.1 %collective-permute-start.6 = (bf16[128,1280]{1,0:T(8,128)(2,1)}, bf16[128,1280]{1,0:T(8,128)(2,1)S(1)}, u32[]{:S(2)}, u32[]{:S(2)}) collective-permute-start(bf16[128,1280]{1,0:T(8,128)(2,1)} %collective-permute-done.5), channel_id=1, source_target_pairs={{0,1},{1,0},{2,3},{3,2},{4,5},{5,4},{6,7},{7,6},{8,9},{9,8},{10,11... | collective-permute-start | bytes 983048 | tf_op jit(solution)/shard_map/ppermute | solution.py:211
  64.2 7.5 %collective-permute-start.1 = (bf16[128,1280]{1,0:T(8,128)(2,1)}, bf16[128,1280]{1,0:T(8,128)(2,1)S(1)}, u32[]{:S(2)}, u32[]{:S(2)}) collective-permute-start(bf16[128,1280]{1,0:T(8,128)(2,1)} %collective-permute-done), channel_id=1, source_target_pairs={{0,1},{1,0},{2,3},{3,2},{4,5},{5,4},{6,7},{7,6},{8,9},{9,8},{10,11... | collective-permute-start | bytes 983048 | tf_op jit(solution)/shard_map/ppermute | solution.py:211
  66.3 11.8 %slice-start.2 = ((s8[10485760]{0:T(1024)(128)(4,1)}), s8[2097152]{0:T(1024)(128)(4,1)S(1)}, s32[]{:S(2)}) async-start(s8[10485760]{0:T(1024)(128)(4,1)} %bitcast.9), calls=%async_computation.2 | async-start | bytes 4194304
  68.7 34.5 %collective-permute-start.13 = (bf16[128,1024]{1,0:T(8,128)(2,1)S(1)}, bf16[128,1024]{1,0:T(8,128)(2,1)S(1)}, u32[]{:S(2)}, u32[]{:S(2)}) collective-permute-start(bf16[128,1024]{1,0:T(8,128)(2,1)S(1)} %convolution_convert_fusion.rest_2_), channel_id=1, source_target_pairs={{0,8},{2,10},{4,12},{6,14},{8,16},{10,18},{12,20},{14,22},{16,24},... | collective-permute-start | bytes 786440 | tf_op jit(solution)/shard_map/ppermute | solution.py:230
  71.2 32.0 %collective-permute-start.12 = (bf16[128,1024]{1,0:T(8,128)(2,1)S(1)}, bf16[128,1024]{1,0:T(8,128)(2,1)S(1)}, u32[]{:S(2)}, u32[]{:S(2)}) collective-permute-start(bf16[128,1024]{1,0:T(8,128)(2,1)S(1)} %convolution_convert_fusion.1.rest_1_), channel_id=1, source_target_pairs={{0,16},{2,18},{4,20},{6,22},{8,24},{10,26},{12,28},{14,30},{16,0},... | collective-permute-start | bytes 786440 | tf_op jit(solution)/shard_map/ppermute | solution.py:230
  74.1 29.1 %collective-permute-start.11 = (bf16[128,1024]{1,0:T(8,128)(2,1)S(1)}, bf16[128,1024]{1,0:T(8,128)(2,1)S(1)}, u32[]{:S(2)}, u32[]{:S(2)}) collective-permute-start(bf16[128,1024]{1,0:T(8,128)(2,1)S(1)} %convolution_convert_fusion.2.rest_0_), channel_id=1, source_target_pairs={{0,24},{2,26},{4,28},{6,30},{8,0},{10,2},{12,4},{14,6},{16,8},{18,... | collective-permute-start | bytes 786440 | tf_op jit(solution)/shard_map/ppermute | solution.py:230

commit v4 on v3

--- a/solution.py
+++ b/solution.py
@@ -230,10 +230,8 @@
         received.append(lax.ppermute(sent[-1], "rep", shift(outer - d)))
 
     stale = jnp.dot(normed, old_kv.reshape(width, both), preferred_element_type=jnp.float32)
-    early = 3 * rows // 8
-    held = cached_attention(queries, key_cache, value_cache, lengths, 0, early, [], ())
     qr, acc, stat = cached_attention(
-        queries, key_cache, value_cache, lengths, early, rows - early, sent, held
+        queries, key_cache, value_cache, lengths, 0, rows, sent, ()
     )
     norm = jnp.broadcast_to(norm, (flat, HEAD))
     attended, keys, values = final_attention(adopt, qr, acc, stat, norm, stale, own, received)

time: 114 us -> 91.4 us (0.80)
  local copies, waits for them, and re-layouts: 28.7 us -> 17.7 us
  matrix products: 11 us -> 4.58 us
  Pallas kernels: 43.4 us -> 41.3 us
  starting transfers between devices: 19.8 us -> 18.1 us
  waiting for transfers between devices: 6.22 us -> 4.95 us
    ppermute x3, waiting for transfers between devices: 6.19 us -> 0.93 us  [on_device(): block = lax.ppermute(block, ('rep', 'tp'), holders(d))]
    dynamic_update_slice x3, local copies, waits for them, and re-layouts: 5.97 us -> 1.23 us  [on_device(): weights = lax.dynamic_update_slice(weights, got, ((spot ^ k) * count, 0))]
    dot_general x3, matrix products: 7.15 us -> 2.51 us  [on_device(): partial = jnp.dot(inputs[d], weights, preferred_element_type=jnp.float32)]
    ppermute x3, waiting for transfers between devices: 0.01 us -> 4 us  [on_device(): got = lax.ppermute(piece, 'rep', [(r, r ^ k) for r in range(replicas)])]
    ppermute x3, starting transfers between devices: 9.99 us -> 7.26 us  [on_device(): block = lax.ppermute(block, ('rep', 'tp'), holders(d))]
    unnamed x18, local copies, waits for them, and re-layouts: 16.9 us -> 14.1 us
    pallas_call x2 -> x1, Pallas kernels: 34.9 us -> 32.8 us  [cached_attention(): pl.pallas_call(functools.partial(cached_kernel, start), grid_spec=pltpu.P...]
    dynamic_update_slice x1, local copies, waits for them, and re-layouts: 1.99 us -> 0.06 us  [on_device(): weights = lax.dynamic_update_slice(weights, piece, (spot * count, 0))]
  transfers between devices with their start and end apart: 14 -> 14, of which waited for: 1 -> 2; matrix products, arithmetic and copies ran while one was open for 31% -> 23% of each run, Pallas kernels for 31% -> 36%
where the time goes in v4:
time: 91.4 us; the launch traced here: 91 us
  Pallas kernels  41.3 us (45%)
  starting transfers between devices  18.1 us (20%)
  local copies, waits for them, and re-layouts  17.7 us (19%)
  waiting for transfers between devices  4.95 us (5%)
  matrix products  4.58 us (5%)
  other arithmetic  2.63 us (3%)
  between operations  1.7 us (2%)
    pallas_call x1, Pallas kernels, cached_attention(): pl.pallas_call(functools.partial(cached_kernel, start), grid_spec=pltpu.P...  32.8 us
    unnamed x18, local copies, waits for them, and re-layouts  14.1 us
    pallas_call x1, Pallas kernels, final_attention(): pl.pallas_call(final_kernel, grid_spec=pltpu.PrefetchScalarGridSpec(num_s...  8.49 us
    ppermute x3, starting transfers between devices, on_device(): block = lax.ppermute(block, ('rep', 'tp'), holders(d))  7.26 us
    ppermute x3, starting transfers between devices, on_device(): received.append(lax.ppermute(sent[-1], 'rep', shift(outer - d)))  4.94 us
    ppermute x3, starting transfers between devices, on_device(): got = lax.ppermute(piece, 'rep', [(r, r ^ k) for r in range(replicas)])  4.55 us
    ppermute x3, waiting for transfers between devices, on_device(): got = lax.ppermute(piece, 'rep', [(r, r ^ k) for r in range(replicas)])  4 us
    dot_general x3, matrix products, on_device(): partial = jnp.dot(inputs[d], weights, preferred_element_type=jnp.float32)  2.51 us
  transfers between devices with their start and end apart: 14, of which 2 were waited for; matrix products, arithmetic and copies ran while one was open for 23% of the time, Pallas kernels for 36%

profile of v4, /device:TPU:0, one launch (start us, length us, event | category | flops | bytes accessed | tf_op | source)
XLA Modules:
  0.0 91.0 jit_solution(15932133101729798547)
XLA Ops:
  0.6 1.2 %copy.12 = bf16[40,8,2,512]{3,1,2,0:T(8,128)(2,1)S(1)} copy(bf16[40,8,2,512]{3,2,1,0:T(2,128)(2,1)} %bitcast.19) | data formatting | bytes 1310720
  1.8 3.0 %collective-permute-start.2 = (bf16[320,1024]{1,0:T(8,128)(2,1)S(1)}, bf16[320,1024]{1,0:T(8,128)(2,1)}, u32[]{:S(2)}, u32[]{:S(2)}) collective-permute-start(bf16[320,1024]{1,0:T(8,128)(2,1)S(1)} %bitcast.15), channel_id=1, source_target_pairs={{0,2},{2,0},{4,6},{6,4},{8,10},{10,8},{12,14},{14,12},{16,18},{18,... | collective-permute-start | bytes 1966088 | tf_op jit(solution)/shard_map/ppermute | solution.py:181
  4.8 1.5 %collective-permute-start.3 = (bf16[320,1024]{1,0:T(8,128)(2,1)S(1)}, bf16[320,1024]{1,0:T(8,128)(2,1)S(1)}, u32[]{:S(2)}, u32[]{:S(2)}) collective-permute-start(bf16[320,1024]{1,0:T(8,128)(2,1)S(1)} %bitcast.16), channel_id=1, source_target_pairs={{0,4},{2,6},{4,0},{6,2},{8,12},{10,14},{12,8},{14,10},{16,20},{18,... | collective-permute-start | bytes 1966088 | tf_op jit(solution)/shard_map/ppermute | solution.py:181
  6.4 1.5 %reshape.26 = bf16[128,2560]{1,0:T(8,128)(2,1)S(1)} reshape(bf16[32,4,2560]{2,1,0:T(4,128)(2,1)} %param.8) | data formatting | bytes 1310720 | tf_op jit(solution)/shard_map/reshape | solution.py:184
  7.9 1.0 %dynamic-slice_select_fusion = (bf16[128,1280]{1,0:T(8,128)(2,1)S(1)}, bf16[128,1280]{1,0:T(8,128)(2,1)}, bf16[128,1280]{1,0:T(8,128)(2,1)}, bf16[128,1280]{1,0:T(8,128)(2,1)}) fusion(bf16[128,2560]{1,0:T(8,128)(2,1)S(1)} %reshape.26, s32[]{:T(128)S(6)} %select_n.65, pred[]{:T(512)S(6)} %eq.5, s32[]{:T(128)S(6)} %select_n.60, s32[]{:T(128)S(6)} %select_n.59, ...), kind=kLoop, calls=%fused_computation.11 | loop fusion | flops 163840 | bytes 2621457 | tf_op jit(solution)/shard_map/jit(_where)/select_n | solution.py:206
  8.9 1.3 %collective-permute-start.7 = (bf16[128,1280]{1,0:T(8,128)(2,1)}, bf16[128,1280]{1,0:T(8,128)(2,1)}, u32[]{:S(2)}, u32[]{:S(2)}) collective-permute-start(bf16[128,1280]{1,0:T(8,128)(2,1)} %get-tuple-element.15), channel_id=1, source_target_pairs={{1,25},{3,27},{5,29},{7,31},{8,0},{10,2},{12,4},{14,6},{16,8},{18,... | collective-permute-start | bytes 983048 | tf_op jit(solution)/shard_map/ppermute | solution.py:208
  10.2 1.3 %collective-permute-start.5 = (bf16[128,1280]{1,0:T(8,128)(2,1)}, bf16[128,1280]{1,0:T(8,128)(2,1)S(1)}, u32[]{:S(2)}, u32[]{:S(2)}) collective-permute-start(bf16[128,1280]{1,0:T(8,128)(2,1)} %get-tuple-element.16), channel_id=1, source_target_pairs={{1,17},{3,19},{5,21},{7,23},{9,25},{11,27},{13,29},{15,31},{16,0},... | collective-permute-start | bytes 983048 | tf_op jit(solution)/shard_map/ppermute | solution.py:208
  11.5 11.4 %copy.13 = bf16[640,8,2,512]{3,1,2,0:T(8,128)(2,1)} copy(bf16[640,8,2,512]{3,2,1,0:T(2,128)(2,1)} %bitcast.14) | data formatting | bytes 20971520
  23.6 0.1 broadcast_in_dim.16
  23.8 0.7 copy-done.2
  24.5 4.7 %collective-permute-start = (bf16[128,1280]{1,0:T(8,128)(2,1)S(1)}, bf16[128,1280]{1,0:T(8,128)(2,1)S(1)}, u32[]{:S(2)}, u32[]{:S(2)}) collective-permute-start(bf16[128,1280]{1,0:T(8,128)(2,1)S(1)} %copy-done.2), channel_id=1, source_target_pairs={{0,8},{2,10},{4,12},{6,14},{9,17},{11,19},{13,21},{15,23},{17,25},... | collective-permute-start | bytes 983048 | tf_op jit(solution)/shard_map/ppermute | solution.py:208
  29.2 0.3 broadcast_in_dim.15
  29.6 0.3 collective-permute-start.8
  29.9 1.1 %constant_dynamic-update-slice_fusion.4 = bf16[1280,1024]{1,0:T(8,128)(2,1)S(1)} fusion(bf16[1280,1024]{1,0:T(8,128)(2,1)S(1)} %constant_dynamic-update-slice_fusion.5, bf16[320,1024]{1,0:T(8,128)(2,1)} %collective-permute-done.2, s32[]{:T(128)S(6)} %select_n.56), kind=kLoop, calls=%fused_computation.22 | loop fusion | bytes 1310724 | tf_op jit(solution)/shard_map/dynamic_update_slice | solution.py:182
  31.1 4.0 %collective-permute-done.3 = bf16[320,1024]{1,0:T(8,128)(2,1)S(1)} collective-permute-done((bf16[320,1024]{1,0:T(8,128)(2,1)S(1)}, bf16[320,1024]{1,0:T(8,128)(2,1)S(1)}, u32[]{:S(2)}, u32[]{:S(2)}) %collective-permute-start.3) | collective-permute-done | bytes 655392 | tf_op jit(solution)/shard_map/ppermute | solution.py:181
  35.1 0.6 collective-permute-start.10
  35.7 0.9 %collective-permute-done = bf16[128,1280]{1,0:T(8,128)(2,1)S(1)} collective-permute-done((bf16[128,1280]{1,0:T(8,128)(2,1)S(1)}, bf16[128,1280]{1,0:T(8,128)(2,1)S(1)}, u32[]{:S(2)}, u32[]{:S(2)}) %collective-permute-start) | collective-permute-done | bytes 327712 | tf_op jit(solution)/shard_map/ppermute | solution.py:208
  36.6 0.5 collective-permute-start.1
  37.2 1.5 %convolution_convert_fusion.rest_2_ = bf16[128,1024]{1,0:T(8,128)(2,1)S(1)} fusion(bf16[1280,1024]{1,0:T(8,128)(2,1)S(1)} %constant_dynamic-update-slice_fusion.2, bf16[128,1280]{1,0:T(8,128)(2,1)} %collective-permute-done.7, bf16[128,1280]{1,0:T(8,128)(2,1)S(1)} %collective-permute-done.8), kind=kOutput, calls=%fused_computation.6 | convolution fusion | flops 335839232 | bytes 3538944 | tf_op jit(solution)/shard_map/dot_general | solution.py:228
  38.7 0.7 collective-permute-start.13
  39.4 0.5 convolution_convert_fusion.1.rest_1_
  39.9 2.7 %collective-permute-start.12 = (bf16[128,1024]{1,0:T(8,128)(2,1)S(1)}, bf16[128,1024]{1,0:T(8,128)(2,1)S(1)}, u32[]{:S(2)}, u32[]{:S(2)}) collective-permute-start(bf16[128,1024]{1,0:T(8,128)(2,1)S(1)} %convolution_convert_fusion.1.rest_1_), channel_id=1, source_target_pairs={{0,16},{2,18},{4,20},{6,22},{8,24},{10,26},{12,28},{14,30},{16,0},... | collective-permute-start | bytes 786440 | tf_op jit(solution)/shard_map/ppermute | solution.py:230
  42.7 0.3 fusion
  43.0 0.5 convolution_convert_fusion.2.rest_0_
  43.6 1.6 %collective-permute-start.11 = (bf16[128,1024]{1,0:T(8,128)(2,1)S(1)}, bf16[128,1024]{1,0:T(8,128)(2,1)S(1)}, u32[]{:S(2)}, u32[]{:S(2)}) collective-permute-start(bf16[128,1024]{1,0:T(8,128)(2,1)S(1)} %convolution_convert_fusion.2.rest_0_), channel_id=1, source_target_pairs={{0,24},{2,26},{4,28},{6,30},{8,0},{10,2},{12,4},{14,6},{16,8},{18,... | collective-permute-start | bytes 786440 | tf_op jit(solution)/shard_map/ppermute | solution.py:230
  45.2 1.6 %fusion.2.sk.sv = f32[128,1024]{1,0:T(8,128)S(1)} fusion(bf16[5120,1024]{1,0:T(8,128)(2,1)S(1)} %bitcast.13, bf16[128,5120]{1,0:T(8,128)(2,1)S(1)} %constant_dynamic-update-slice_fusion, f32[128]{0:T(128)S(1)} %add_rsqrt_fusion), kind=kOutput, calls=%fused_computation.4 | convolution fusion | flops 1344143360 | bytes 12321280 | tf_op jit(solution)/shard_map/dot_general | solution.py:232
  46.8 0.6 slice-done.1
  47.4 0.2 copy-done
  47.6 32.8 %shard_map.95 = (bf16[32,4,32,128]{3,2,1,0:T(8,128)(2,1)S(1)}, f32[32,4,32,128]{3,2,1,0:T(8,128)S(1)}, f32[32,4,32,128]{3,2,1,0:T(8,128)S(1)}) custom-call(s32[32]{0:T(128)S(1)} %copy-done.1, bf16[32,4,4096]{2,1,0:T(4,128)(2,1)S(1)} %copy-done, bf16[32,256,512]{2,1,0:T(8,128)(2,1)S(1)} %bitcast.10, bf16[32,256,512]{2,1,0:T(8,128)(2,1)} %v_ref.1, ...), custom_call_target="tpu_custom_call" | custom-call | flops 536870912 | bytes 24117248 | tf_op jit(solution)/shard_map/pallas_call | solution.py:60
  80.4 0.5 fusion.5.ok.ov
  81.1 8.5 %shard_map.96 = (bf16[32,4,4096]{2,1,0:T(4,128)(2,1)}, bf16[128,512]{1,0:T(8,128)(2,1)S(1)}, bf16[128,512]{1,0:T(8,128)(2,1)S(1)}) custom-call(s32[1]{0:T(128)S(6)} %copy.20.adopt, bf16[32,4,32,128]{3,2,1,0:T(8,128)(2,1)S(1)} %get-tuple-element.8.qr_ref, f32[32,4,32,128]{3,2,1,0:T(8,128)S(1)} %get-tuple-element.9.acc_ref, ...), custom_call_target="tpu_custom_call" | custom-call | flops 268435456 | bytes 6291456 | tf_op jit(solution)/shard_map/pallas_call | solution.py:141
  89.7 1.3 %pad_maximum_fusion = bf16[32,4,2,512]{3,2,1,0:T(2,128)(2,1)} fusion(bf16[32,4,1,512]{3,2,1,0:T(2,128)(2,1)S(1)} %stack.13, bf16[32,4,1,512]{3,2,1,0:T(2,128)(2,1)S(1)} %stack.12), kind=kLoop, calls=%fused_computation.15 | loop fusion | flops 524288 | bytes 524288 | tf_op jit(solution)/shard_map/stack | solution.py:238
  (39 shorter events, 0.6 us)
Async XLA Ops:
  1.8 27.8 %collective-permute-start.2 = (bf16[320,1024]{1,0:T(8,128)(2,1)S(1)}, bf16[320,1024]{1,0:T(8,128)(2,1)}, u32[]{:S(2)}, u32[]{:S(2)}) collective-permute-start(bf16[320,1024]{1,0:T(8,128)(2,1)S(1)} %bitcast.15), channel_id=1, source_target_pairs={{0,2},{2,0},{4,6},{6,4},{8,10},{10,8},{12,14},{14,12},{16,18},{18,... | collective-permute-start | bytes 1966088 | tf_op jit(solution)/shard_map/ppermute | solution.py:181
  4.8 30.2 %collective-permute-start.3 = (bf16[320,1024]{1,0:T(8,128)(2,1)S(1)}, bf16[320,1024]{1,0:T(8,128)(2,1)S(1)}, u32[]{:S(2)}, u32[]{:S(2)}) collective-permute-start(bf16[320,1024]{1,0:T(8,128)(2,1)S(1)} %bitcast.16), channel_id=1, source_target_pairs={{0,4},{2,6},{4,0},{6,2},{8,12},{10,14},{12,8},{14,10},{16,20},{18,... | collective-permute-start | bytes 1966088 | tf_op jit(solution)/shard_map/ppermute | solution.py:181
  6.3 30.3 %collective-permute-start.4 = (bf16[320,1024]{1,0:T(8,128)(2,1)S(1)}, bf16[320,1024]{1,0:T(8,128)(2,1)S(1)}, u32[]{:S(2)}, u32[]{:S(2)}) collective-permute-start(bf16[320,1024]{1,0:T(8,128)(2,1)S(1)} %bitcast.17), channel_id=1, source_target_pairs={{0,6},{2,4},{4,2},{6,0},{8,14},{10,12},{12,10},{14,8},{16,22},{18,... | collective-permute-start | bytes 1966088 | tf_op jit(solution)/shard_map/ppermute | solution.py:181
  8.9 14.9 %collective-permute-start.7 = (bf16[128,1280]{1,0:T(8,128)(2,1)}, bf16[128,1280]{1,0:T(8,128)(2,1)}, u32[]{:S(2)}, u32[]{:S(2)}) collective-permute-start(bf16[128,1280]{1,0:T(8,128)(2,1)} %get-tuple-element.15), channel_id=1, source_target_pairs={{1,25},{3,27},{5,29},{7,31},{8,0},{10,2},{12,4},{14,6},{16,8},{18,... | collective-permute-start | bytes 983048 | tf_op jit(solution)/shard_map/ppermute | solution.py:208
  10.2 25.0 %collective-permute-start.5 = (bf16[128,1280]{1,0:T(8,128)(2,1)}, bf16[128,1280]{1,0:T(8,128)(2,1)S(1)}, u32[]{:S(2)}, u32[]{:S(2)}) collective-permute-start(bf16[128,1280]{1,0:T(8,128)(2,1)} %get-tuple-element.16), channel_id=1, source_target_pairs={{1,17},{3,19},{5,21},{7,23},{9,25},{11,27},{13,29},{15,31},{16,0},... | collective-permute-start | bytes 983048 | tf_op jit(solution)/shard_map/ppermute | solution.py:208
  23.6 1.0 %copy-start.2 = (bf16[128,1280]{1,0:T(8,128)(2,1)S(1)}, bf16[128,1280]{1,0:T(8,128)(2,1)}, u32[]{:S(2)}) copy-start(bf16[128,1280]{1,0:T(8,128)(2,1)} %get-tuple-element.17) | copy-start | bytes 983044
  23.7 21.5 %slice-start.2 = ((s8[10485760]{0:T(1024)(128)(4,1)}), s8[4194304]{0:T(1024)(128)(4,1)S(1)}, s32[]{:S(2)}) async-start(s8[10485760]{0:T(1024)(128)(4,1)} %bitcast.11), calls=%async_computation.2 | async-start | bytes 8388608
  24.5 12.1 %collective-permute-start = (bf16[128,1280]{1,0:T(8,128)(2,1)S(1)}, bf16[128,1280]{1,0:T(8,128)(2,1)S(1)}, u32[]{:S(2)}, u32[]{:S(2)}) collective-permute-start(bf16[128,1280]{1,0:T(8,128)(2,1)S(1)} %copy-done.2), channel_id=1, source_target_pairs={{0,8},{2,10},{4,12},{6,14},{9,17},{11,19},{13,21},{15,23},{17,25},... | collective-permute-start | bytes 983048 | tf_op jit(solution)/shard_map/ppermute | solution.py:208
  29.6 7.6 %collective-permute-start.8 = (bf16[128,1280]{1,0:T(8,128)(2,1)}, bf16[128,1280]{1,0:T(8,128)(2,1)S(1)}, u32[]{:S(2)}, u32[]{:S(2)}) collective-permute-start(bf16[128,1280]{1,0:T(8,128)(2,1)} %collective-permute-done.7), channel_id=1, source_target_pairs={{0,1},{1,0},{2,3},{3,2},{4,5},{5,4},{6,7},{7,6},{8,9},{9,8},{10,11... | collective-permute-start | bytes 983048 | tf_op jit(solution)/shard_map/ppermute | solution.py:211
  31.1 14.1 %slice-start.3 = ((s8[10485760]{0:T(1024)(128)(4,1)}), s8[4194304]{0:T(1024)(128)(4,1)S(1)}, s32[]{:S(2)}) async-start(s8[10485760]{0:T(1024)(128)(4,1)} %bitcast.11), calls=%async_computation.3 | async-start | bytes 8388608
  35.1 7.5 %collective-permute-start.9 = (bf16[128,2560]{1,0:T(8,128)(2,1)S(1)}, bf16[128,2560]{1,0:T(8,128)(2,1)S(1)}, u32[]{:S(2)}, u32[]{:S(2)}) collective-permute-start(bf16[128,2560]{1,0:T(8,128)(2,1)S(1)} %reshape.26), channel_id=1, source_target_pairs={{0,1},{1,0},{2,3},{3,2},{4,5},{5,4},{6,7},{7,6},{8,9},{9,8},{10,11... | collective-permute-start | bytes 1966088 | tf_op jit(solution)/shard_map/ppermute | solution.py:218
  35.1 45.3 %collective-permute-start.10 = (bf16[128,1280]{1,0:T(8,128)(2,1)S(1)}, bf16[128,1280]{1,0:T(8,128)(2,1)S(1)}, u32[]{:S(2)}, u32[]{:S(2)}) collective-permute-start(bf16[128,1280]{1,0:T(8,128)(2,1)S(1)} %get-tuple-element.14), channel_id=1, source_target_pairs={{0,1},{1,0},{2,3},{3,2},{4,5},{5,4},{6,7},{7,6},{8,9},{9,8},{10,11... | collective-permute-start | bytes 983048 | tf_op jit(solution)/shard_map/ppermute | solution.py:211
  36.6 2.8 %collective-permute-start.6 = (bf16[128,1280]{1,0:T(8,128)(2,1)S(1)}, bf16[128,1280]{1,0:T(8,128)(2,1)S(1)}, u32[]{:S(2)}, u32[]{:S(2)}) collective-permute-start(bf16[128,1280]{1,0:T(8,128)(2,1)S(1)} %collective-permute-done.5), channel_id=1, source_target_pairs={{0,1},{1,0},{2,3},{3,2},{4,5},{5,4},{6,7},{7,6},{8,9},{9,8},{10,11... | collective-permute-start | bytes 983048 | tf_op jit(solution)/shard_map/ppermute | solution.py:211
  36.6 6.4 %collective-permute-start.1 = (bf16[128,1280]{1,0:T(8,128)(2,1)S(1)}, bf16[128,1280]{1,0:T(8,128)(2,1)S(1)}, u32[]{:S(2)}, u32[]{:S(2)}) collective-permute-start(bf16[128,1280]{1,0:T(8,128)(2,1)S(1)} %collective-permute-done), channel_id=1, source_target_pairs={{0,1},{1,0},{2,3},{3,2},{4,5},{5,4},{6,7},{7,6},{8,9},{9,8},{10,11... | collective-permute-start | bytes 983048 | tf_op jit(solution)/shard_map/ppermute | solution.py:211
  38.7 6.5 %slice-start.4 = ((s8[10485760]{0:T(1024)(128)(4,1)}), s8[2097152]{0:T(1024)(128)(4,1)S(1)}, s32[]{:S(2)}) async-start(s8[10485760]{0:T(1024)(128)(4,1)} %bitcast.11), calls=%async_computation.4 | async-start | bytes 4194304
  38.7 42.2 %collective-permute-start.13 = (bf16[128,1024]{1,0:T(8,128)(2,1)S(1)}, bf16[128,1024]{1,0:T(8,128)(2,1)S(1)}, u32[]{:S(2)}, u32[]{:S(2)}) collective-permute-start(bf16[128,1024]{1,0:T(8,128)(2,1)S(1)} %convolution_convert_fusion.rest_2_), channel_id=1, source_target_pairs={{0,8},{2,10},{4,12},{6,14},{8,16},{10,18},{12,20},{14,22},{16,24},... | collective-permute-start | bytes 786440 | tf_op jit(solution)/shard_map/ppermute | solution.py:230
  39.9 41.0 %collective-permute-start.12 = (bf16[128,1024]{1,0:T(8,128)(2,1)S(1)}, bf16[128,1024]{1,0:T(8,128)(2,1)S(1)}, u32[]{:S(2)}, u32[]{:S(2)}) collective-permute-start(bf16[128,1024]{1,0:T(8,128)(2,1)S(1)} %convolution_convert_fusion.1.rest_1_), channel_id=1, source_target_pairs={{0,16},{2,18},{4,20},{6,22},{8,24},{10,26},{12,28},{14,30},{16,0},... | collective-permute-start | bytes 786440 | tf_op jit(solution)/shard_map/ppermute | solution.py:230
  43.0 3.7 %slice-start = ((s8[8388608]{0:T(1024)(128)(4,1)}), s8[4194304]{0:T(1024)(128)(4,1)S(1)}, s32[]{:S(2)}) async-start(s8[8388608]{0:T(1024)(128)(4,1)} %bitcast.9), calls=%async_computation | async-start | bytes 8388608
  43.6 37.4 %collective-permute-start.11 = (bf16[128,1024]{1,0:T(8,128)(2,1)S(1)}, bf16[128,1024]{1,0:T(8,128)(2,1)S(1)}, u32[]{:S(2)}, u32[]{:S(2)}) collective-permute-start(bf16[128,1024]{1,0:T(8,128)(2,1)S(1)} %convolution_convert_fusion.2.rest_0_), channel_id=1, source_target_pairs={{0,24},{2,26},{4,28},{6,30},{8,0},{10,2},{12,4},{14,6},{16,8},{18,... | collective-permute-start | bytes 786440 | tf_op jit(solution)/shard_map/ppermute | solution.py:230
  45.2 2.2 %slice-start.1 = ((s8[8388608]{0:T(1024)(128)(4,1)}), s8[4194304]{0:T(1024)(128)(4,1)S(1)}, s32[]{:S(2)}) async-start(s8[8388608]{0:T(1024)(128)(4,1)} %bitcast.9), calls=%async_computation.1 | async-start | bytes 8388608
  45.2 2.4 %copy-start = (bf16[32,4,4096]{2,1,0:T(4,128)(2,1)S(1)}, bf16[32,4,4096]{2,1,0:T(4,128)(2,1)}, u32[]{:S(2)}) copy-start(bf16[32,4,4096]{2,1,0:T(4,128)(2,1)} %q_ref.1) | copy-start | bytes 3145732
  45.2 2.4 %copy-start.1 = (s32[32]{0:T(128)S(1)}, s32[32]{0:T(128)}, u32[]{:S(2)}) copy-start(s32[32]{0:T(128)} %lengths.1) | copy-start | bytes 388
